TPU v7x, 256 devices: a whole 4x4x8 slice. The times are simulated.
256 devices in a mesh: dp: 4 (over z_lo), ctx: 64 (over y, z_hi, x, core).
Axes of the slice: x: 4, y: 4, z: 8 (z_hi: 2, z_lo: 4; z = z_hi * 4 + z_lo), core: 2. Of those that a mesh axis runs over, the one named last changes fastest.
Arguments:
- queries: bfloat16 [4, 8192, 1536], P('dp', 'ctx'), may hold values from -16 to 16
- values: bfloat16 [4, 8192, 1536], P('dp', 'ctx'), may hold values from -6 to 6
- out_grad: bfloat16 [4, 8192, 1536], P('dp', 'ctx'), may hold values from -6 to 6
- out_weight: bfloat16 [1536, 1536], replicated, may hold values from -0.15625 to 0.15625
- filter_spec: bfloat16 [2, 8192, 1536], P(None, 'ctx'), may hold values from -6 to 6
Outputs:
- grad_queries: bfloat16 [4, 8192, 1536], P('dp', 'ctx')
- grad_values: bfloat16 [4, 8192, 1536], P('dp', 'ctx')
- grad_filter: float32 [2, 8192, 1536], P(None, 'ctx')
- grad_weight: float32 [1536, 1536], P('ctx')
All inputs are finite; a program needn't handle non-finite values.
Results may differ from a plain program's by a relative error of at most 0.014.
Values may be sent and summed in bfloat16 or wider, within the bound.
A program may use at most 128 MiB of HBM per device.

v0:
```python
import math

import jax
import jax.numpy as jnp
from jax import lax
from jax.sharding import PartitionSpec as P

PRECISE = lax.Precision.HIGHEST


def angle_pair(product, period):
    angles = (product % period).astype(jnp.float32) * (2.0 * math.pi / period)
    return (jnp.cos(angles), jnp.sin(angles))


def dot_exact(matrix, operand):
    return jnp.dot(matrix, operand, precision=PRECISE, preferred_element_type=jnp.float32)


def on_device(queries, values, out_grad, out_weight, filter_spec):
    blocks = lax.axis_size("ctx")
    copies = lax.axis_size("dp")
    block_index = lax.axis_index("ctx")
    tok_rows = queries.shape[1]
    channels = queries.shape[2]
    block_share = tok_rows // blocks
    seq_length = tok_rows * blocks
    block_ids = jnp.arange(blocks, dtype=jnp.int32)
    row_ids = jnp.arange(tok_rows, dtype=jnp.int32)
    cross_cos, cross_sin = angle_pair(block_ids[:, None] * block_ids[None, :], blocks)
    local_cos, local_sin = angle_pair(row_ids[:, None] * row_ids[None, :], tok_rows)
    held_rows = block_index * block_share + jnp.arange(block_share, dtype=jnp.int32)
    twist_cos, twist_sin = angle_pair(block_ids[:, None] * held_rows[None, :], seq_length)
    twist_cos = twist_cos[:, :, None]
    twist_sin = twist_sin[:, :, None]
    undo_cos, undo_sin = angle_pair(block_index * row_ids, seq_length)
    undo_cos = undo_cos[:, None]
    undo_sin = undo_sin[:, None]

    def first_section(blocked):
        flattened = blocked.reshape(blocks, -1)
        real_part = dot_exact(cross_cos, flattened).reshape(blocked.shape)
        imag_part = -dot_exact(cross_sin, flattened).reshape(blocked.shape)
        return jnp.stack(
            [
                real_part * twist_cos + imag_part * twist_sin,
                imag_part * twist_cos - real_part * twist_sin,
            ]
        )

    def last_section(gathered):
        real_part = gathered[0, 0]
        imag_part = gathered[1, 0]
        return jnp.stack(
            [
                dot_exact(local_cos, real_part) + dot_exact(local_sin, imag_part),
                dot_exact(local_cos, imag_part) - dot_exact(local_sin, real_part),
            ]
        )

    def spectrum(sectioned):
        return last_section(
            lax.all_to_all(sectioned, "ctx", split_axis=1, concat_axis=2, tiled=True)
        )

    def inverse_last(gathered):
        out_shape = gathered.shape[1:]
        real_part = gathered[0].reshape(blocks, -1)
        imag_part = gathered[1].reshape(blocks, -1)
        result = (dot_exact(cross_cos, real_part) - dot_exact(cross_sin, imag_part)) / seq_length
        return result.reshape(out_shape)

    def inverse(spec_real, spec_imag):
        real_part = dot_exact(local_cos, spec_real) - dot_exact(local_sin, spec_imag)
        imag_part = dot_exact(local_cos, spec_imag) + dot_exact(local_sin, spec_real)
        sectioned = jnp.stack(
            [
                real_part * undo_cos - imag_part * undo_sin,
                imag_part * undo_cos + real_part * undo_sin,
            ]
        )[:, None]
        return inverse_last(
            lax.all_to_all(sectioned, "ctx", split_axis=2, concat_axis=1, tiled=True)
        )

    filter_real = filter_spec[0].astype(jnp.float32)
    filter_imag = filter_spec[1].astype(jnp.float32)
    query_rows = queries[0]
    value_rows = values[0]
    grad_rows = out_grad[0]
    value_spec = spectrum(
        first_section(
            lax.all_to_all(
                value_rows.reshape(blocks, block_share, channels),
                "ctx",
                split_axis=0,
                concat_axis=0,
                tiled=True,
            ).astype(jnp.float32)
        )
    )
    grad_gated = lax.dot_general(
        grad_rows, out_weight, (((1,), (1,)), ((), ())), preferred_element_type=jnp.float32
    )
    value_real = value_spec[0]
    value_imag = value_spec[1]
    mixed_blocks = inverse(
        filter_real * value_real - filter_imag * value_imag,
        filter_real * value_imag + filter_imag * value_real,
    )
    mixed_rows = lax.all_to_all(
        mixed_blocks, "ctx", split_axis=0, concat_axis=1, tiled=True
    ).reshape(tok_rows, channels)
    query_float = query_rows.astype(jnp.float32)
    gated_rows = (query_float * mixed_rows).astype(jnp.bfloat16)
    grad_query = (grad_gated * mixed_rows).astype(jnp.bfloat16)
    grad_mixed = grad_gated * query_float
    grad_sectioned = first_section(
        lax.all_to_all(
            grad_mixed.reshape(blocks, block_share, channels),
            "ctx",
            split_axis=0,
            concat_axis=0,
            tiled=True,
        )
    )
    grad_spec = spectrum(grad_sectioned)
    grad_real = grad_spec[0]
    grad_imag = grad_spec[1]
    filter_term = (
        jnp.stack(
            [
                grad_real * value_real + grad_imag * value_imag,
                grad_imag * value_real - grad_real * value_imag,
            ]
        )
        / seq_length
    )
    grad_filter = lax.psum(filter_term.astype(jnp.bfloat16), "dp").astype(jnp.float32)
    back_blocks = inverse(
        grad_real * filter_real + grad_imag * filter_imag,
        grad_imag * filter_real - grad_real * filter_imag,
    ).astype(jnp.bfloat16)
    scale_factor = 1.0 / math.sqrt(copies * seq_length)
    weight_sum = lax.psum(
        lax.psum_scatter(
            lax.dot_general(
                gated_rows, grad_rows, (((0,), (0,)), ((), ())), preferred_element_type=jnp.float32
            ),
            "ctx",
            scatter_dimension=0,
            tiled=True,
        ).astype(jnp.bfloat16),
        "dp",
    ).astype(jnp.float32)
    grad_weight = weight_sum * scale_factor
    query_out = grad_query[None]
    value_out = lax.all_to_all(back_blocks, "ctx", split_axis=0, concat_axis=1, tiled=True)
    return (query_out, value_out, grad_filter, grad_weight)


def solution(mesh):
    return jax.shard_map(
        on_device,
        mesh=mesh,
        in_specs=(
            P("dp", "ctx", None),
            P("dp", "ctx", None),
            P("dp", "ctx", None),
            P(),
            P(None, "ctx", None),
        ),
        out_specs=(
            P("dp", "ctx", None),
            P("dp", "ctx", None),
            P(None, "ctx", None),
            P("ctx", None),
        ),
        check_vma=False,
    )
```

profile of v0, /device:TPU:1, one launch (start us, length us, event | category | flops | bytes accessed | tf_op | source)
XLA Modules:
  0.0 499.9 jit_solution(15400104797184578834)
XLA Ops:
  7.2 1.9 reshape_squeeze.15
  9.1 15.6 %all-to-all-start = ((bf16[64,2,1536]{2,1,0:T(2,128)(2,1)}), bf16[64,2,1536]{2,1,0:T(2,128)(2,1)S(1)}, u32[]{:S(2)}, u32[]{:S(2)}) async-start(bf16[64,2,1536]{2,1,0:T(2,128)(2,1)} %reshape_squeeze.15), calls=%async_computation | async-start | bytes 786432 | tf_op jit(solution)/shard_map/all_to_all | solution.py:93
  24.9 15.0 %all-to-all-done = bf16[64,2,1536]{2,1,0:T(2,128)(2,1)S(1)} async-done(((bf16[64,2,1536]{2,1,0:T(2,128)(2,1)}), bf16[64,2,1536]{2,1,0:T(2,128)(2,1)S(1)}, u32[]{:S(2)}, u32[]{:S(2)}) %all-to-all-start) | async-done | bytes 393248 | tf_op jit(solution)/shard_map/all_to_all | solution.py:93
  41.3 2.4 copy.19
  43.7 6.3 %all-to-all-start.1 = ((f32[2,64,2,1536]{3,2,0,1:T(2,128)}), f32[2,64,2,1536]{3,2,0,1:T(2,128)S(1)}, u32[]{:S(2)}, u32[]{:S(2)}) async-start(f32[2,64,2,1536]{3,2,0,1:T(2,128)} %copy.19), calls=%async_computation.1 | async-start | bytes 3145728 | tf_op jit(solution)/shard_map/all_to_all | solution.py:63
  50.0 39.6 %all-to-all-done.1 = f32[2,64,2,1536]{3,2,0,1:T(2,128)S(1)} async-done(((f32[2,64,2,1536]{3,2,0,1:T(2,128)}), f32[2,64,2,1536]{3,2,0,1:T(2,128)S(1)}, u32[]{:S(2)}, u32[]{:S(2)}) %all-to-all-start.1) | async-done | bytes 1572896 | tf_op jit(solution)/shard_map/all_to_all | solution.py:63
  101.4 47.1 %all_to_all.67 = f32[2,1,128,1536]{3,0,1,2:T(2,128)S(1)} all-to-all(f32[2,1,128,1536]{3,0,1,2:T(2,128)S(1)} %copy.20), channel_id=1, replica_groups=mesh['dp'=4,'ctx'=64] {'ctx'}, dimensions={2} | all-to-all | bytes 3145728 | tf_op jit(solution)/shard_map/all_to_all | solution.py:83
  148.5 5.0 slice_reduce_fusion.2
  158.5 4.2 all-to-all-start.3
  164.7 15.4 %all-to-all-done.3 = f32[64,2,1536]{2,1,0:T(2,128)S(1)} async-done(((f32[64,2,1536]{2,1,0:T(2,128)}), f32[64,2,1536]{2,1,0:T(2,128)S(1)}, u32[]{:S(2)}, u32[]{:S(2)}) %all-to-all-start.3) | async-done | bytes 786464 | tf_op jit(solution)/shard_map/all_to_all | solution.py:111
  182.4 5.1 %fusion.17 = f32[1536,1536]{1,0:T(8,128)} fusion(bf16[128,1536]{1,0:T(8,128)(2,1)S(1)} %convert_element_type.140, bf16[1,128,1536]{2,1,0:T(8,128)(2,1)S(1)} %copy-done), kind=kOutput, calls=%fused_computation.59 | convolution fusion | flops 603979776 | bytes 10223616 | tf_op jit(solution)/shard_map/dot_general | solution.py:147
  188.0 4.8 bitcast_multiply_fusion
  193.3 27.4 %all_to_all.68 = f32[64,2,1536]{2,1,0:T(2,128)S(1)} all-to-all(f32[64,2,1536]{2,1,0:T(2,128)S(1)} %reshape.165), channel_id=1, replica_groups=mesh['dp'=4,'ctx'=64] {'ctx'}, dimensions={0} | all-to-all | bytes 1572864 | tf_op jit(solution)/shard_map/all_to_all | solution.py:119
  224.1 29.8 %all_to_all.69 = f32[2,64,2,1536]{3,2,0,1:T(2,128)S(1)} all-to-all(f32[2,64,2,1536]{3,2,0,1:T(2,128)S(1)} %copy.23), channel_id=1, replica_groups=mesh['dp'=4,'ctx'=64] {'ctx'}, dimensions={1} | all-to-all | bytes 3145728 | tf_op jit(solution)/shard_map/all_to_all | solution.py:63
  255.5 1.7 squeeze.21
  266.6 2.4 copy.24
  268.9 19.9 %all-to-all-start.6 = ((f32[2,1,128,1536]{3,0,1,2:T(2,128)}), f32[2,1,128,1536]{3,0,1,2:T(2,128)}, u32[]{:S(2)}, u32[]{:S(2)}) async-start(f32[2,1,128,1536]{3,0,1,2:T(2,128)} %copy.24), calls=%async_computation.6 | async-start | bytes 3145728 | tf_op jit(solution)/shard_map/all_to_all | solution.py:83
  290.1 58.5 %all-to-all-done.6 = f32[2,1,128,1536]{3,0,1,2:T(2,128)} async-done(((f32[2,1,128,1536]{3,0,1,2:T(2,128)}), f32[2,1,128,1536]{3,0,1,2:T(2,128)}, u32[]{:S(2)}, u32[]{:S(2)}) %all-to-all-start.6) | async-done | bytes 1572896 | tf_op jit(solution)/shard_map/all_to_all | solution.py:83
  348.7 6.2 %slice_reduce_fusion = (f32[128,1536]{1,0:T(8,128)S(1)}, f32[128,1536]{1,0:T(8,128)S(1)}) fusion(f32[2,1,128,1536]{3,0,1,2:T(2,128)} %all-to-all-done.6), kind=kLoop, calls=%fused_computation.36 | loop fusion | bytes 3145728 | tf_op jit(solution)/shard_map/slice | solution.py:69
  356.4 66.3 %reduce-scatter.2.cloned.1.call-done = f32[24,1536]{1,0:T(8,128)} async-done(((f32[1536,1536]{1,0:T(8,128)}), f32[24,1536]{1,0:T(8,128)}) %reduce-scatter.2.cloned.1.call-update) | async-done | bytes 147472 | tf_op jit(solution)/shard_map/reduce_scatter | solution.py:146
  425.5 28.4 %all_to_all.70 = bf16[64,2,1536]{2,1,0:T(2,128)(2,1)S(1)} all-to-all(bf16[64,2,1536]{2,1,0:T(2,128)(2,1)S(1)} %convert_element_type.134), channel_id=1, replica_groups=mesh['dp'=4,'ctx'=64] {'ctx'}, dimensions={0} | all-to-all | bytes 786432 | tf_op jit(solution)/shard_map/all_to_all | solution.py:158
  454.8 34.0 %all-reduce.3.cloned.1.call-done = (bf16[2,128,1536]{2,1,0:T(8,128)(2,1)}, bf16[24,1536]{1,0:T(8,128)(2,1)}) async-done(((bf16[2,128,1536]{2,1,0:T(8,128)(2,1)}, bf16[24,1536]{1,0:T(8,128)(2,1)}), (bf16[2,128,1536]{2,1,0:T(8,128)(2,1)}, bf16[24,1536]{1,0:T(8,128)(2,1)})) %all-reduce.3.cloned.1.call-update) | async-done | bytes 860176 | tf_op jit(solution)/shard_map/psum | solution.py:139
  488.8 1.6 convert_multiply_fusion.8
  490.4 2.5 convert_element_type.136
  (69 shorter events, 44.1 us)
Async XLA Ops:
  7.2 175.2 %copy-start = (bf16[1,128,1536]{2,1,0:T(8,128)(2,1)S(1)}, bf16[1,128,1536]{2,1,0:T(8,128)(2,1)}, u32[]{:S(2)}) copy-start(bf16[1,128,1536]{2,1,0:T(8,128)(2,1)} %param.7) | copy-start | bytes 1179652
  9.1 30.7 %all-to-all-start = ((bf16[64,2,1536]{2,1,0:T(2,128)(2,1)}), bf16[64,2,1536]{2,1,0:T(2,128)(2,1)S(1)}, u32[]{:S(2)}, u32[]{:S(2)}) async-start(bf16[64,2,1536]{2,1,0:T(2,128)(2,1)} %reshape_squeeze.15), calls=%async_computation | async-start | bytes 786432 | tf_op jit(solution)/shard_map/all_to_all | solution.py:93
  43.7 46.0 %all-to-all-start.1 = ((f32[2,64,2,1536]{3,2,0,1:T(2,128)}), f32[2,64,2,1536]{3,2,0,1:T(2,128)S(1)}, u32[]{:S(2)}, u32[]{:S(2)}) async-start(f32[2,64,2,1536]{3,2,0,1:T(2,128)} %copy.19), calls=%async_computation.1 | async-start | bytes 3145728 | tf_op jit(solution)/shard_map/all_to_all | solution.py:63
  94.1 1.1 copy-start.2
  158.5 21.5 %all-to-all-start.3 = ((f32[64,2,1536]{2,1,0:T(2,128)}), f32[64,2,1536]{2,1,0:T(2,128)S(1)}, u32[]{:S(2)}, u32[]{:S(2)}) async-start(f32[64,2,1536]{2,1,0:T(2,128)} %reshape.163), calls=%async_computation.3 | async-start | bytes 1572864 | tf_op jit(solution)/shard_map/all_to_all | solution.py:111
  162.8 259.9 %reduce-scatter.2.cloned.1.call-start = ((), (), s32[]{:S(2)}) async-start(), calls=%async_computation.9 | async-start | bytes 9584640 | tf_op jit(solution)/shard_map/reduce_scatter | solution.py:146
  257.2 1.1 copy-start.4
  259.3 1.1 copy-start.5
  260.5 1.1 copy-start.3
  268.9 79.8 %all-to-all-start.6 = ((f32[2,1,128,1536]{3,0,1,2:T(2,128)}), f32[2,1,128,1536]{3,0,1,2:T(2,128)}, u32[]{:S(2)}, u32[]{:S(2)}) async-start(f32[2,1,128,1536]{3,0,1,2:T(2,128)} %copy.24), calls=%async_computation.6 | async-start | bytes 3145728 | tf_op jit(solution)/shard_map/all_to_all | solution.py:83
  288.9 200.0 %all-reduce.3.cloned.1.call-start = ((), (), s32[]{:S(2)}) async-start(), calls=%async_computation.10 | async-start | bytes 1720320 | tf_op jit(solution)/shard_map/psum | solution.py:139
  425.4 67.4 %copy-start.1 = (bf16[1,128,1536]{2,1,0:T(8,128)(2,1)S(1)}, bf16[1,128,1536]{2,1,0:T(8,128)(2,1)}, u32[]{:S(2)}) copy-start(bf16[1,128,1536]{2,1,0:T(8,128)(2,1)} %param.7) | copy-start | bytes 1179652
Sparse Core Ops, SparseCore 0:
  187.6 234.9 reduce-scatter.1
  426.2 62.6 all-reduce.2
where the time goes:
time: 505 us; the launch traced here: 500 us
  waiting for transfers between devices  229 us (45%)
  blocking collectives  133 us (26%)
  starting transfers between devices  46.5 us (9%)
  matrix products  35.1 us (7%)
  local copies, waits for them, and re-layouts  33.4 us (7%)
  between operations  14.7 us (3%)
  other arithmetic  8.54 us (2%)
    reduce_scatter x1, waiting for transfers between devices, on_device(): lax.psum_scatter(lax.dot_general(gated_rows, grad_rows, (((0,), (0,)), ((...  66.3 us
    all_to_all x1, waiting for transfers between devices, inverse(): lax.all_to_all(sectioned, 'ctx', split_axis=2, concat_axis=1, tiled=True)  58.5 us
    all_to_all x1, blocking collectives, inverse(): lax.all_to_all(sectioned, 'ctx', split_axis=2, concat_axis=1, tiled=True)  47.1 us
    all_to_all x1, waiting for transfers between devices, spectrum(): lax.all_to_all(sectioned, 'ctx', split_axis=1, concat_axis=2, tiled=True)  39.6 us
    psum x1, waiting for transfers between devices, on_device(): lax.psum(filter_term.astype(jnp.bfloat16), 'dp').astype(jnp.float32)  34 us
    all_to_all x1, blocking collectives, spectrum(): lax.all_to_all(sectioned, 'ctx', split_axis=1, concat_axis=2, tiled=True)  29.8 us
    all_to_all x1, blocking collectives, on_device(): lax.all_to_all(back_blocks, 'ctx', split_axis=0, concat_axis=1, tiled=True)  28.4 us
    all_to_all x1, blocking collectives, on_device(): lax.all_to_all(grad_mixed.reshape(blocks, block_share, channels), 'ctx',...  27.4 us
  transfers between devices with their start and end apart: 6, of which 6 were waited for; matrix products, arithmetic and copies ran while one was open for 7% of the time, Pallas kernels for 0%

commit v1 on v0

v1 whole, which is shorter than its diff:
```python
import functools
import math

import jax
import jax.numpy as jnp
import numpy as np
from jax import lax
from jax.experimental import pallas as pl
from jax.experimental.pallas import tpu as pltpu
from jax.sharding import PartitionSpec as P

F32 = jnp.float32
BF16 = jnp.bfloat16
TOK = 128
D = 1536
SEQ = 8192
SLOTS = 33
ROWS = SLOTS * 16
MESH = pl.DeviceIdType.MESH


def slot_of(k):
    if k == 32:
        return 16
    if k % 4 == 0:
        return k // 4
    if k % 4 == 2:
        return 8 + k // 4
    return 17 + k // 4


HELD = [k for k in range(64) if k % 4 == 1 or (k % 2 == 0 and k <= 32)]


def tables():
    r = np.arange(TOK)
    angle = 2.0 * math.pi * ((r[:, None] * r[None, :]) % TOK) / TOK
    c, s = np.cos(angle), np.sin(angle)
    forward = np.block([[c, -s], [s, c]])
    inverse = np.block([[c, s], [-s, c]])

    def halves(m):
        hi = m.astype(np.float32).astype(jnp.bfloat16)
        lo = (m - hi.astype(np.float64)).astype(np.float32).astype(jnp.bfloat16)
        return np.stack([hi, lo])

    twist = np.zeros((2, 40, TOK), np.float32)
    for k in HELD:
        a = 2.0 * math.pi * k * r / SEQ
        twist[0, slot_of(k)] = np.cos(a)
        twist[1, slot_of(k)] = np.sin(a)
    return halves(forward), halves(inverse), twist


def p_add(a, b):
    if a is None:
        return b
    return a if b is None else a + b


def p_sub(a, b):
    if b is None:
        return a
    return -b if a is None else a - b


def c_add(a, b):
    return (p_add(a[0], b[0]), p_add(a[1], b[1]))


def c_sub(a, b):
    return (p_sub(a[0], b[0]), p_sub(a[1], b[1]))


def by_i(a):
    return (p_sub(None, a[1]), a[0])


def p_mul(a, f):
    return None if a is None or f == 0.0 else a * f


def turn(z, k, n):
    k = k % n
    if k == 0:
        return z
    if 4 * k == n:
        return by_i(z)
    if 2 * k == n:
        return c_sub((None, None), z)
    if 4 * k == 3 * n:
        return (z[1], p_sub(None, z[0]))
    c, s = math.cos(2 * math.pi * k / n), math.sin(2 * math.pi * k / n)
    return (
        p_sub(p_mul(z[0], c), p_mul(z[1], s)),
        p_add(p_mul(z[0], s), p_mul(z[1], c)),
    )


def four(z, sign):
    t0, t1 = c_add(z[0], z[2]), c_sub(z[0], z[2])
    t2, t3 = c_add(z[1], z[3]), by_i(c_sub(z[1], z[3]))
    if sign < 0:
        return [c_add(t0, t2), c_sub(t1, t3), c_sub(t0, t2), c_add(t1, t3)]
    return [c_add(t0, t2), c_add(t1, t3), c_sub(t0, t2), c_sub(t1, t3)]


def blocks_forward(get, put):
    t = {}
    for h in range(2):
        for c in range(2):
            for x in range(4):
                v = [get(h, c, y, x) for y in range(4)]
                s02, d02 = v[0] + v[2], v[0] - v[2]
                s13, d13 = v[1] + v[3], v[1] - v[3]
                a = 8 * h + 2 * x + c
                t[0, h, c, x] = (s02 + s13, None)
                t[1, h, c, x] = turn((d02, -d13), -a, 64)
                t[2, h, c, x] = turn((s02 - s13, None), -2 * a, 64)
    for ky in range(3):
        for kh in range(2):
            halves = []
            for c in range(2):
                z = []
                for x in range(4):
                    if kh == 0:
                        z.append(c_add(t[ky, 0, c, x], t[ky, 1, c, x]))
                    else:
                        z.append(turn(c_sub(t[ky, 0, c, x], t[ky, 1, c, x]), -(2 * x + c), 16))
                z = four(z, -1)
                if c == 1:
                    z = [turn(z[kx], -kx, 8) for kx in range(4)]
                halves.append(z)
            for kx in range(4):
                k = ky + 4 * kh + 8 * kx
                put(slot_of(k), c_add(halves[0][kx], halves[1][kx]))
                if ky == 1 or k == 0:
                    put(slot_of(k + 32), c_sub(halves[0][kx], halves[1][kx]))


def blocks_inverse(get, put):
    u = {}
    for ky in range(3):
        for kh in range(2):
            lanes = [[], []]
            for kx in range(4):
                k = ky + 4 * kh + 8 * kx
                z = get(slot_of(k))
                if ky == 1 or k == 0:
                    w = get(slot_of(k + 32))
                    first, second = c_add(z, w), c_sub(z, w)
                else:
                    first, second = z, z
                lanes[0].append(first)
                lanes[1].append(turn(second, kx, 8))
            for c in range(2):
                z = four(lanes[c], 1)
                for x in range(4):
                    u[ky, kh, c, x] = turn(z[x], (2 * x + c) * kh, 16)
    for c in range(2):
        for x in range(4):
            for h in range(2):
                a = 8 * h + 2 * x + c
                join = c_add if h == 0 else c_sub
                u0 = join(u[0, 0, c, x], u[0, 1, c, x])[0]
                u1 = turn(join(u[1, 0, c, x], u[1, 1, c, x]), a, 64)
                u2 = turn(join(u[2, 0, c, x], u[2, 1, c, x]), 2 * a, 64)[0]
                even, odd = u0 + u2, u0 - u2
                put(h, c, 0, x, even + u1[0])
                put(h, c, 1, x, odd - u1[1])
                put(h, c, 2, x, even - u1[0])
                put(h, c, 3, x, odd + u1[1])


def split(v):
    hi = v.astype(BF16)
    return hi, (v - hi.astype(F32)).astype(BF16)


def dot(a, b):
    return jnp.dot(a, b, preferred_element_type=F32)


def dot_t(a, b):
    return lax.dot_general(a, b, (((1,), (1,)), ((), ())), preferred_element_type=F32)


def dot3(hi, lo, m):
    return dot(hi, m[0]) + dot(lo, m[0]) + dot(hi, m[1])


def kernel(
    values, queries, out_grad, weight, filt, m_fwd, m_inv, twist,
    o_query, o_value, o_filter, o_weight,
    w_in, og_x, g_gated, qt, val_t, gm_t, fil_t,
    r1v, r1g, f1, xv, xg, hx, hrev, hs, lhi, llo, spec_v, spec_g, back,
    ymix, ygv, r2m, r2v, mix_t, gv_t, gp, gpx, gs, gr, gfi,
    gat, gat_x, wa, ra0, ra1, sb0, sb1, rb0, rb1, sc, rc, sd, rd,
    s_w, s_ogs, s_ogr, s_gts, s_gtr, s_gps, s_gpr,
    s1vs, s1vr, s1gs, s1gr, s1fs, s1fr,
    s2vs, s2vr, s2gs, s2gr, s2fs, s2fr, s3fs, s3fr,
    sams, samr, savs, savr, sbms, sbmr, sbvs, sbvr,
    sags, sagr, sbgs, sbgr,
    sras, srar, srbs, srbr, srcs, srcr, srds, srdr,
):
    n = lax.axis_index("dp")
    ctx = lax.axis_index("ctx")
    y, h = lax.div(ctx, 16), lax.rem(lax.div(ctx, 8), 2)
    x, c = lax.rem(lax.div(ctx, 2), 4), lax.rem(ctx, 2)
    p, z = y * 4 + x, h * 4 + n
    hc = h * 2 + c
    active = n != 2
    unit = z - (z >= 3).astype(jnp.int32) - (z >= 7).astype(jnp.int32)

    def at(pp, zz, cc):
        return (
            lax.rem(zz, 4),
            lax.div(pp, 4) * 16 + lax.div(zz, 4) * 8 + lax.rem(pp, 4) * 2 + cc,
        )

    def remote(src, dst, ss, rs, dev):
        return pltpu.make_async_remote_copy(
            src_ref=src, dst_ref=dst, send_sem=ss, recv_sem=rs,
            device_id=dev, device_id_type=MESH,
        )

    def local(src, dst, sem):
        pltpu.make_async_copy(src, dst, sem).start()

    def landed(dst, sem):
        pltpu.make_async_copy(dst, dst, sem).wait()

    def left(src, sem):
        pltpu.make_async_copy(src, src, sem).wait()

    def rounds(lo, hi, body):
        lax.fori_loop(lo, hi, lambda i, carry: (body(i), carry)[1], 0)

    def over_p(send):
        rounds(1, 16, lambda i: send(lax.rem(p + i, 16)))

    weight_copy = pltpu.make_async_copy(weight, w_in, s_w)
    weight_copy.start()

    barrier = pltpu.get_barrier_semaphore()

    def greet_p(q):
        pl.semaphore_signal(barrier, inc=1, device_id=at(q, z, c), device_id_type=MESH)

    over_p(greet_p)

    def greet_z(i):
        zz = lax.rem(z + lax.div(i, 2), 8)
        cc = lax.rem(c + lax.rem(i, 2), 2)
        pl.semaphore_signal(barrier, inc=1, device_id=at(p, zz, cc), device_id_type=MESH)

    rounds(1, 16, greet_z)

    def turn_in(src, dst):
        for j in range(D // 128):
            dst[j * 128 : (j + 1) * 128, :] = src[:, j * 128 : (j + 1) * 128].T

    turn_in(values, val_t)
    pl.semaphore_wait(barrier, 30)

    def hop1(src, dst, ss, rs):
        local(src.at[pl.ds(p * 96, 96)], dst.at[p], rs.at[p])
        over_p(
            lambda q: remote(
                src.at[pl.ds(q * 96, 96)], dst.at[p], ss.at[q], rs.at[p], at(q, z, c)
            ).start()
        )

    def hop1_done(src, ss):
        over_p(lambda q: left(src.at[pl.ds(q * 96, 96)], ss.at[q]))

    hop1(val_t, r1v, s1vs, s1vr)

    other = at(p, z, 1 - c)
    lanes_other = pl.ds(pl.multiple_of((1 - c) * 768, 768), 768)
    lanes_own = pl.ds(pl.multiple_of(c * 768, 768), 768)
    og_copy = remote(out_grad.at[:, lanes_other], og_x, s_ogs, s_ogr, other)
    og_copy.start()

    for part in range(2):
        turn_in(filt.at[part], fil_t.at[part])
    two = jnp.logical_or(n == 0, n == 3)
    sz = [
        lax.rem(z + 3 * (n == 2).astype(jnp.int32), 8),
        lax.rem(z + 8 + (n == 3).astype(jnp.int32) - (n == 0).astype(jnp.int32), 8),
    ]

    def unit_at(zz):
        return zz - (zz >= 3).astype(jnp.int32) - (zz >= 7).astype(jnp.int32)

    def f_src(k, q):
        return fil_t.at[:, pl.ds(q * 96 + unit_at(sz[k]) * 16, 16), :]

    def filter_hop1(k):
        local(f_src(k, p), f1.at[k, p], s1fr.at[k, p])
        over_p(
            lambda q: remote(
                f_src(k, q), f1.at[k, p], s1fs.at[k, q], s1fr.at[k, p], at(q, z, c)
            ).start()
        )

    filter_hop1(0)
    pl.when(two)(lambda: filter_hop1(1))

    def hop2(r1, r1_sem, dst, ss, rs):
        rounds(0, 16, lambda q: landed(r1.at[q], r1_sem.at[q]))
        core = lax.div(n, 2)
        slot = dst.at[lax.rem(n, 2), hc]

        def send(i):
            u = lax.rem(unit + i, 6)
            zz = u + (u >= 2).astype(jnp.int32) + (u >= 5).astype(jnp.int32)
            src = r1.at[:, pl.ds(u * 16, 16), :]
            mine = jnp.logical_and(zz == z, core == c)
            sem = rs.at[lax.rem(n, 2), hc]

            @pl.when(mine)
            def _():
                local(src, slot, sem)

            @pl.when(jnp.logical_not(mine))
            def _():
                remote(src, slot, ss.at[u], sem, at(p, zz, core)).start()

        rounds(0, 6, send)

    def hop2_done(r1, ss):
        core = lax.div(n, 2)

        def done(u):
            zz = u + (u >= 2).astype(jnp.int32) + (u >= 5).astype(jnp.int32)
            mine = jnp.logical_and(zz == z, core == c)

            @pl.when(jnp.logical_not(mine))
            def _():
                left(r1.at[:, pl.ds(u * 16, 16), :], ss.at[u])

        rounds(0, 6, done)

    hop2(r1v, s1vr, xv, s2vs, s2vr)

    def filter_hop2(k):
        rounds(0, 16, lambda q: landed(f1.at[k, q], s1fr.at[k, q]))
        mine = sz[k] == z

        @pl.when(mine)
        def _():
            local(f1.at[k], hx.at[h, c], s2fr.at[h])

        @pl.when(jnp.logical_not(mine))
        def _():
            remote(f1.at[k], hx.at[h, c], s2fs.at[k], s2fr.at[h], at(p, sz[k], c)).start()

    def filter_hop2_done(k):
        @pl.when(sz[k] != z)
        def _():
            left(f1.at[k], s2fs.at[k])

    filter_hop2(0)
    pl.when(two)(lambda: filter_hop2(1))

    turn_in(queries, qt)
    weight_copy.wait()

    def gated_rows(i):
        rows = pl.ds(pl.multiple_of(i * 256, 256), 256)
        g = dot_t(w_in[rows, :], out_grad[...])
        g_gated[rows, :] = g
        gm_t[rows, :] = (g * qt[rows, :].astype(F32)).astype(BF16)

    rounds(0, 6, gated_rows)
    hop1(gm_t, r1g, s1gs, s1gr)

    def transform(src, spec):
        def one(nn):
            def get(hh, cc, yy, xx):
                return src[nn, 2 * hh + cc, 4 * yy + xx].astype(F32)

            def put(s, v):
                co, si = twist[0, s : s + 1, :], twist[1, s : s + 1, :]
                re, im = v
                if im is None:
                    out = (re * co, -(re * si))
                else:
                    out = (re * co + im * si, im * co - re * si)
                for j in range(2):
                    hi, lo = split(out[j])
                    lhi[s * 16 : s * 16 + 16, j * 128 : j * 128 + 128] = hi
                    llo[s * 16 : s * 16 + 16, j * 128 : j * 128 + 128] = lo

            blocks_forward(get, put)
            spec[nn] = dot3(lhi[...], llo[...], m_fwd)

        rounds(0, 2, one)

    def untransform(product, dst):
        def one(nn):
            re, im = product(nn)
            for j, v in enumerate((re, im)):
                hi, lo = split(v)
                lhi[:, j * 128 : j * 128 + 128] = hi
                llo[:, j * 128 : j * 128 + 128] = lo
            back[...] = dot3(lhi[...], llo[...], m_inv)

            def get(s):
                co = twist[0, s : s + 1, :] * (1.0 / SEQ)
                si = twist[1, s : s + 1, :] * (1.0 / SEQ)
                re = back[s * 16 : s * 16 + 16, :128]
                im = back[s * 16 : s * 16 + 16, 128:]
                return (re * co - im * si, im * co + re * si)

            def put(hh, cc, yy, xx, v):
                dst[nn, 2 * hh + cc, 4 * yy + xx] = v.astype(BF16)

            blocks_inverse(get, put)

        rounds(0, 2, one)

    def hop_a(src, dst, ss, rs):
        def send(i):
            nn, hh, cc = lax.div(i, 4), lax.rem(lax.div(i, 2), 2), lax.rem(i, 2)
            zz = hh * 4 + 2 * c + nn
            mine = jnp.logical_and(zz == z, cc == c)

            @pl.when(mine)
            def _():
                local(src.at[nn, 2 * hh + cc], dst.at[unit], rs.at[unit])

            @pl.when(jnp.logical_not(mine))
            def _():
                remote(
                    src.at[nn, 2 * hh + cc], dst.at[unit], ss.at[i], rs.at[unit], at(p, zz, cc)
                ).start()

        rounds(0, 8, send)

    def hop_a_done(src, ss):
        def done(i):
            nn, hh, cc = lax.div(i, 4), lax.rem(lax.div(i, 2), 2), lax.rem(i, 2)
            zz = hh * 4 + 2 * c + nn
            mine = jnp.logical_and(zz == z, cc == c)

            @pl.when(jnp.logical_not(mine))
            def _():
                left(src.at[nn, 2 * hh + cc], ss.at[i])

        rounds(0, 8, done)

    def hop_b(r2, r2_sem, dst, ss, rs):
        rounds(0, 6, lambda u: landed(r2.at[u], r2_sem.at[u]))
        local(r2.at[:, p], dst.at[p], rs.at[p])
        over_p(
            lambda q: remote(r2.at[:, q], dst.at[p], ss.at[q], rs.at[p], at(q, z, c)).start()
        )

    def hop_b_done(r2, ss):
        over_p(lambda q: left(r2.at[:, q], ss.at[q]))

    ident = (
        lax.broadcasted_iota(jnp.int32, (128, 128), 0)
        == lax.broadcasted_iota(jnp.int32, (128, 128), 1)
    ).astype(F32).astype(BF16)
    flip = (
        lax.broadcasted_iota(jnp.int32, (128, 128), 0)
        == 127 - lax.broadcasted_iota(jnp.int32, (128, 128), 1)
    ).astype(F32).astype(BF16)

    @pl.when(active)
    def _():
        for hh in range(2):
            landed(hx.at[hh, c], s2fr.at[hh])
            remote(hx.at[hh, c], hx.at[hh, c], s3fs.at[hh], s3fr.at[hh], other).start()
        rounds(0, 8, lambda i: landed(xv.at[lax.div(i, 4), lax.rem(i, 4)],
                                      s2vr.at[lax.div(i, 4), lax.rem(i, 4)]))
        transform(xv, spec_v)

    hop2(r1g, s1gr, xg, s2gs, s2gr)

    @pl.when(active)
    def _():
        for hh in range(2):
            landed(hx.at[hh, 1 - c], s3fr.at[hh])

        def raw(k):
            return hx[(k >> 3) & 1, k & 1, (k >> 4) * 4 + ((k >> 1) & 3)]

        for k in HELD:
            s = slot_of(k)
            if k % 32:
                hrev[s * 32 : s * 32 + 32, :] = raw(64 - k).reshape(32, 128)
            else:
                hrev[s * 32 : s * 32 + 32, :] = jnp.zeros((32, 128), BF16)
        turned = dot(hrev[...], flip).reshape(SLOTS, 32, 128)
        for k in HELD:
            s = slot_of(k)
            v = raw(k).astype(F32)
            hs[s * 16 : s * 16 + 16, :128] = v[0] + turned[s, :16]
            hs[s * 16 : s * 16 + 16, 128:] = v[1] - turned[s, 16:]

        def mixed_product(nn):
            hr, hi = hs[:, :128], hs[:, 128:]
            vr, vi = spec_v[nn, :, :128], spec_v[nn, :, 128:]
            return hr * vr - hi * vi, hr * vi + hi * vr

        untransform(mixed_product, ymix)
        hop_a(ymix, r2m, sams, samr)
        rounds(0, 8, lambda i: landed(xg.at[lax.div(i, 4), lax.rem(i, 4)],
                                      s2gr.at[lax.div(i, 4), lax.rem(i, 4)]))
        transform(xg, spec_g)

        def value_product(nn):
            hr, hi = hs[:, :128], hs[:, 128:]
            gr_, gi = spec_g[nn, :, :128], spec_g[nn, :, 128:]
            return gr_ * hr + gi * hi, gi * hr - gr_ * hi

        untransform(value_product, ygv)
        hop_a(ygv, r2v, savs, savr)

        re, im = 0.0, 0.0
        for nn in range(2):
            vr, vi = spec_v[nn, :, :128], spec_v[nn, :, 128:]
            gr_, gi = spec_g[nn, :, :128], spec_g[nn, :, 128:]
            re = re + (gr_ * vr + gi * vi)
            im = im + (gi * vr - gr_ * vi)
        gp[:, :128] = re * (1.0 / SEQ)
        gp[:, 128:] = im * (1.0 / SEQ)
        gp_rows = pl.ds(pl.multiple_of((1 - c) * 256, 256), 272)
        remote(gp.at[gp_rows], gpx, s_gps, s_gpr, other).start()

    hop_b(r2m, samr, mix_t, sbms, sbmr)

    @pl.when(active)
    def _():
        landed(gpx, s_gpr)

        def fill(i):
            q, hh = lax.div(i, 2), lax.rem(i, 2)
            a = lax.div(q, 4) * 16 + hh * 8 + lax.rem(q, 4) * 2 + c
            low = lax.rem(a, 4)
            straight = jnp.logical_or(low == 1, jnp.logical_and(c == 0, a <= 32))
            k = jnp.where(straight, a, 64 - a)
            base = jnp.where(lax.rem(k, 4) == 1, 17, jnp.where(lax.rem(k, 4) == 2, 8, 0))
            s = jnp.where(k == 32, 16, base + lax.div(k, 4))
            total = gp[pl.ds(pl.multiple_of(s * 16, 16), 16), :] + gpx[
                pl.ds(pl.multiple_of(s * 16 - 256 * c, 16), 16), :
            ]
            gs[q, hh, 0] = total[:, :128].astype(BF16)
            gs[q, hh, 1] = total[:, 128:].astype(BF16)

        rounds(0, 32, fill)
        local(gs.at[p], gr.at[p], sagr.at[p])
        over_p(
            lambda q: remote(gs.at[q], gr.at[p], sags.at[q], sagr.at[p], at(q, z, c)).start()
        )

    rounds(0, 16, lambda q: landed(mix_t.at[q], sbmr.at[q]))
    mixed = mix_t[...].reshape(D, TOK).astype(F32)
    gat[...] = (qt[...].astype(F32) * mixed).astype(BF16)
    gat_copy = remote(gat, gat_x, s_gts, s_gtr, other)
    gat_copy.start()
    gq = (g_gated[...] * mixed).astype(BF16)
    o_query[...] = dot_t(ident, gq).astype(BF16)

    og_copy.wait_recv()
    gat_copy.wait_recv()

    def weight_rows(i):
        yy, hh = lax.div(i, 2), lax.rem(i, 2)
        rows = pl.ds(pl.multiple_of(i * 192, 192), 192)
        w = dot(gat[rows, :], out_grad[:, lanes_own]) + dot(gat_x[rows, :], og_x[...])
        for part in range(2):
            wa[part, yy, hh] = (
                w[:, part * 384 : (part + 1) * 384].astype(BF16).reshape(4, 48, 384)
            )

    rounds(0, 8, weight_rows)

    def ra_send(i):
        xx, yy = lax.rem(x + i, 4), lax.rem(y + i, 4)
        remote(wa.at[0, :, :, xx], ra0.at[x], sras.at[0, i], srar.at[0, x],
               at(y * 4 + xx, z, c)).start()
        remote(wa.at[1, yy], ra1.at[y], sras.at[1, i], srar.at[1, y],
               at(yy * 4 + x, z, c)).start()

    rounds(1, 4, ra_send)

    hop_b(r2v, savr, gv_t, sbvs, sbvr)

    @pl.when(active)
    def _():
        rounds(0, 16, lambda q: landed(gr.at[q], sagr.at[q]))

        def send(i):
            hh, nn = lax.rem(i, 2), lax.rem(lax.div(i, 2) + n, 4)
            zz = hh * 4 + nn
            sem = sbgr.at[unit]

            @pl.when(zz == z)
            def _():
                local(gr.at[:, hh], gfi.at[:, unit], sem)

            @pl.when(zz != z)
            def _():
                remote(gr.at[:, hh], gfi.at[:, unit], sbgs.at[zz], sem, at(p, zz, c)).start()

        rounds(0, 8, send)

    def ra_wait(i):
        xx, yy = lax.rem(x + i, 4), lax.rem(y + i, 4)
        landed(ra0.at[xx], srar.at[0, xx])
        landed(ra1.at[yy], srar.at[1, yy])

    rounds(1, 4, ra_wait)
    sum0 = wa[0, :, :, x].astype(F32)
    sum1 = wa[1, y].astype(F32)
    for i in range(1, 4):
        sum0 = sum0 + ra0[lax.rem(x + i, 4)].astype(F32)
        sum1 = sum1 + ra1[lax.rem(y + i, 4)].astype(F32)
    sb0[...] = sum0.astype(BF16)
    sb1[...] = sum1.astype(BF16)

    def rb_send(i):
        xx, yy = lax.rem(x + i, 4), lax.rem(y + i, 4)
        remote(sb0.at[yy], rb0.at[y], srbs.at[0, i], srbr.at[0, y], at(yy * 4 + x, z, c)).start()
        remote(sb1.at[:, xx], rb1.at[x], srbs.at[1, i], srbr.at[1, x],
               at(y * 4 + xx, z, c)).start()

    rounds(1, 4, rb_send)

    rounds(0, 16, lambda q: landed(gv_t.at[q], sbvr.at[q]))
    o_value[...] = dot_t(ident, gv_t[...].reshape(D, TOK)).astype(BF16)

    def rb_wait(i):
        xx, yy = lax.rem(x + i, 4), lax.rem(y + i, 4)
        landed(rb0.at[yy], srbr.at[0, yy])
        landed(rb1.at[xx], srbr.at[1, xx])

    rounds(1, 4, rb_wait)
    sum0 = sb0[y].astype(F32)
    sum1 = sb1[:, x].astype(F32)
    for i in range(1, 4):
        sum0 = sum0 + rb0[lax.rem(y + i, 4)].astype(F32)
        sum1 = sum1 + rb1[lax.rem(x + i, 4)].astype(F32)
    sc[:, :, :, :384] = sum0.astype(BF16).reshape(2, 3, 16, 384)
    sc[:, :, :, 384:] = sum1.astype(BF16).reshape(2, 3, 16, 384)

    def rc_send(i):
        hh, t = lax.div(i, 3), lax.rem(i, 3)
        zz = hh * 4 + t

        @pl.when(zz == z)
        def _():
            local(sc.at[hh, t], rc.at[z], srcr.at[z])

        @pl.when(zz != z)
        def _():
            remote(sc.at[hh, t], rc.at[z], srcs.at[i], srcr.at[z], at(p, zz, c)).start()

    rounds(0, 6, rc_send)
    owner = n < 3

    @pl.when(owner)
    def _():
        rounds(0, 8, lambda i: landed(rc.at[i], srcr.at[i]))
        total = rc[0].astype(F32)
        for i in range(1, 8):
            total = total + rc[i].astype(F32)
        sd[...] = total.astype(BF16)

        def send(i):
            nn, cc = lax.div(i, 2), lax.rem(i, 2)
            mine = jnp.logical_and(nn == n, cc == c)

            @pl.when(mine)
            def _():
                local(sd, rd.at[n, c], srdr.at[n, c])

            @pl.when(jnp.logical_not(mine))
            def _():
                remote(sd, rd.at[n, c], srds.at[i], srdr.at[n, c],
                       at(p, h * 4 + nn, cc)).start()

        rounds(0, 8, send)

    def gf_wait(u):
        landed(gfi.at[:, u], sbgr.at[u])

    rounds(0, 6, gf_wait)
    straight = jnp.logical_or(
        lax.rem(ctx, 4) == 1, jnp.logical_and(c == 0, ctx <= 32)
    )
    pick = jnp.where(straight, ident.astype(F32), flip.astype(F32)).astype(BF16)
    sign = jnp.where(straight, 1.0, -1.0)
    o_filter[0] = dot_t(pick, gfi[:, :, 0].reshape(D, TOK))
    o_filter[1] = dot_t(pick, gfi[:, :, 1].reshape(D, TOK)) * sign

    for t in range(3):
        for cc in range(2):
            landed(rd.at[t, cc], srdr.at[t, cc])
    scale = 1.0 / math.sqrt(4 * SEQ)
    for cc in range(2):
        cols = slice(cc * 768, (cc + 1) * 768)

        @pl.when(c == 0)
        def _():
            o_weight[0:16, cols] = rd[0, cc].astype(F32) * scale
            o_weight[16:24, cols] = rd[1, cc].astype(F32)[0:8] * scale

        @pl.when(c == 1)
        def _():
            o_weight[0:8, cols] = rd[1, cc].astype(F32)[8:16] * scale
            o_weight[8:24, cols] = rd[2, cc].astype(F32) * scale

    hop1_done(val_t, s1vs)
    hop1_done(gm_t, s1gs)
    og_copy.wait_send()
    gat_copy.wait_send()
    over_p(lambda q: left(f_src(0, q), s1fs.at[0, q]))
    filter_hop2_done(0)

    @pl.when(two)
    def _():
        over_p(lambda q: left(f_src(1, q), s1fs.at[1, q]))
        filter_hop2_done(1)

    hop2_done(r1v, s2vs)
    hop2_done(r1g, s2gs)
    hop_b_done(r2m, sbms)
    hop_b_done(r2v, sbvs)

    @pl.when(active)
    def _():
        for hh in range(2):
            left(hx.at[hh, c], s3fs.at[hh])
        hop_a_done(ymix, sams)
        hop_a_done(ygv, savs)
        left(gpx, s_gps)
        over_p(lambda q: left(gs.at[q], sags.at[q]))

        def done(zz):
            @pl.when(zz != z)
            def _():
                left(gr.at[:, 0], sbgs.at[zz])

        rounds(0, 8, done)

    def ra_done(i):
        left(ra0.at[0], sras.at[0, i])
        left(ra1.at[0], sras.at[1, i])
        left(rb0.at[0], srbs.at[0, i])
        left(rb1.at[0], srbs.at[1, i])

    rounds(1, 4, ra_done)

    def rc_done(i):
        @pl.when(lax.div(i, 3) * 4 + lax.rem(i, 3) != z)
        def _():
            left(sd, srcs.at[i])

    rounds(0, 6, rc_done)

    @pl.when(owner)
    def _():
        def done(i):
            mine = jnp.logical_and(lax.div(i, 2) == n, lax.rem(i, 2) == c)

            @pl.when(jnp.logical_not(mine))
            def _():
                left(sd, srds.at[i])

        rounds(0, 8, done)


def on_device(queries, values, out_grad, out_weight, filter_spec):
    m_fwd, m_inv, twist = tables()
    vmem = pl.BlockSpec(memory_space=pltpu.VMEM)
    dma = pltpu.SemaphoreType.DMA

    def held(*shape, dtype=BF16):
        return pltpu.VMEM(shape, dtype)

    scratch = [
        held(D, D), held(TOK, 768), held(D, TOK, dtype=F32), held(D, TOK),
        held(D, TOK), held(D, TOK), held(2, D, TOK),
        held(16, 96, TOK), held(16, 96, TOK), held(2, 16, 2, 16, TOK),
        held(2, 4, 16, 16, TOK), held(2, 4, 16, 16, TOK), held(2, 2, 16, 2, 16, TOK),
        held(SLOTS * 32, TOK), held(ROWS, 256, dtype=F32),
        held(ROWS, 256), held(ROWS, 256),
        held(2, ROWS, 256, dtype=F32), held(2, ROWS, 256, dtype=F32), held(ROWS, 256, dtype=F32),
        held(2, 4, 16, 16, TOK), held(2, 4, 16, 16, TOK),
        held(6, 16, 16, TOK), held(6, 16, 16, TOK),
        held(16, 6, 16, TOK), held(16, 6, 16, TOK),
        held(ROWS, 256, dtype=F32), held(272, 256, dtype=F32),
        held(16, 2, 2, 16, TOK), held(16, 2, 2, 16, TOK), held(16, 6, 2, 16, TOK),
        held(D, TOK), held(D, TOK),
        held(2, 4, 2, 4, 48, 384), held(4, 4, 2, 48, 384), held(4, 2, 4, 48, 384),
        held(4, 2, 48, 384), held(2, 4, 48, 384), held(4, 2, 48, 384), held(4, 2, 48, 384),
        held(2, 3, 16, 768), held(8, 16, 768), held(16, 768), held(3, 2, 16, 768),
        dma, dma, dma, dma, dma, dma, dma,
        dma((16,)), dma((16,)), dma((16,)), dma((16,)), dma((2, 16)), dma((2, 16)),
        dma((6,)), dma((2, 4)), dma((6,)), dma((2, 4)), dma((2,)), dma((2,)), dma((2,)), dma((2,)),
        dma((8,)), dma((6,)), dma((8,)), dma((6,)), dma((16,)), dma((16,)), dma((16,)), dma((16,)),
        dma((16,)), dma((16,)), dma((8,)), dma((6,)),
        dma((2, 4)), dma((2, 4)), dma((2, 4)), dma((2, 4)), dma((6,)), dma((8,)),
        dma((8,)), dma((3, 2)),
    ]
    grad_query, grad_value, grad_filter, grad_weight = pl.pallas_call(
        kernel,
        out_shape=(
            jax.ShapeDtypeStruct((TOK, D), BF16),
            jax.ShapeDtypeStruct((TOK, D), BF16),
            jax.ShapeDtypeStruct((2, TOK, D), F32),
            jax.ShapeDtypeStruct((24, D), F32),
        ),
        in_specs=[vmem, vmem, vmem, pl.BlockSpec(memory_space=pl.ANY)] + [vmem] * 4,
        out_specs=(vmem,) * 4,
        scratch_shapes=scratch,
        compiler_params=pltpu.CompilerParams(
            collective_id=0, has_side_effects=True, vmem_limit_bytes=52 * 2**20
        ),
    )(values[0], queries[0], out_grad[0], out_weight, filter_spec,
      jnp.asarray(m_fwd), jnp.asarray(m_inv), jnp.asarray(twist))
    return grad_query[None], grad_value[None], grad_filter, grad_weight


def solution(mesh):
    return jax.shard_map(
        on_device,
        mesh=mesh,
        in_specs=(
            P("dp", "ctx", None),
            P("dp", "ctx", None),
            P("dp", "ctx", None),
            P(),
            P(None, "ctx", None),
        ),
        out_specs=(
            P("dp", "ctx", None),
            P("dp", "ctx", None),
            P(None, "ctx", None),
            P("ctx", None),
        ),
        check_vma=False,
    )
```

time: 505 us -> 118 us (0.23)
  waiting for transfers between devices: 229 us -> 0 us
  blocking collectives: 133 us -> 0 us
  Pallas kernels: 0 us -> 110 us
  starting transfers between devices: 46.5 us -> 0 us
  matrix products: 35.1 us -> 0 us
  local copies, waits for them, and re-layouts: 33.4 us -> 7.01 us
  between operations: 14.7 us -> 0.66 us
  other arithmetic: 8.54 us -> 0 us
    all_to_all x4 -> x0, blocking collectives: 133 us -> none  [the longest x1 47.1 us: inverse(): lax.all_to_all(sectioned, 'ctx', split_axis=2, concat_axis=1, tiled=True)]
    all_to_all x4 -> x0, waiting for transfers between devices: 129 us -> none  [the longest x1 58.5 us: inverse(): lax.all_to_all(sectioned, 'ctx', split_axis=2, concat_axis=1, tiled=True)]
    pallas_call x0 -> x1, Pallas kernels: none -> 110 us  [on_device(): pl.pallas_call(kernel, out_shape=(jax.ShapeDtypeStruct((TOK, D), BF16), j...]
    reduce_scatter x1 -> x0, waiting for transfers between devices: 66.3 us -> none  [on_device(): lax.psum_scatter(lax.dot_general(gated_rows, grad_rows, (((0,), (0,)), ((...]
    all_to_all x4 -> x0, starting transfers between devices: 46.1 us -> none  [the longest x1 19.9 us: inverse(): lax.all_to_all(sectioned, 'ctx', split_axis=2, concat_axis=1, tiled=True)]
    dot_general x26 -> x0, matrix products: 35.1 us -> none  [the longest x24 25.2 us: dot_exact(): jnp.dot(matrix, operand, precision=PRECISE, preferred_element_type=jnp.fl...]
    psum x1 -> x0, waiting for transfers between devices: 34 us -> none  [on_device(): lax.psum(filter_term.astype(jnp.bfloat16), 'dp').astype(jnp.float32)]
    slice x4 -> x0, local copies, waits for them, and re-layouts: 12.3 us -> none  [the longest x2 11.2 us: inverse_last(): imag_part = gathered[1].reshape(blocks, -1)]
  transfers between devices with their start and end apart: 6 -> 0, of which waited for: 6 -> 0; matrix products, arithmetic and copies ran while one was open for 7% -> 0% of each run, Pallas kernels for 0% -> 0%
where the time goes in v1:
time: 118 us
  Pallas kernels  110 us (93%)
  local copies, waits for them, and re-layouts  7.01 us (6%)
    pallas_call x1, Pallas kernels, on_device(): pl.pallas_call(kernel, out_shape=(jax.ShapeDtypeStruct((TOK, D), BF16), j...  110 us
    unnamed x14, local copies, waits for them, and re-layouts  7.01 us

profile of v1, /device:TPU:1, one launch (start us, length us, event | category | flops | bytes accessed | tf_op | source)
XLA Modules:
  0.0 117.8 jit_solution(15224722146671068804)
XLA Ops:
  0.6 0.0 copy-start
  0.6 1.0 copy-done
  1.6 0.0 copy-start.1
  1.6 0.9 copy-done.1
  2.6 0.0 copy-start.2
  2.6 0.9 copy-done.2
  3.5 0.0 copy-start.3
  3.5 0.8 copy-done.3
  4.3 110.2 %shard_map.111 = (bf16[128,1536]{1,0:T(8,128)(2,1)S(1)}, bf16[128,1536]{1,0:T(8,128)(2,1)S(1)}, f32[2,128,1536]{2,1,0:T(8,128)}, f32[24,1536]{1,0:T(8,128)S(1)}) custom-call(bf16[128,1536]{1,0:T(8,128)(2,1)S(1)} %bitcast.5, bf16[128,1536]{1,0:T(8,128)(2,1)} %bitcast.8, bf16[128,1536]{1,0:T(8,128)(2,1)} %bitcast.9, bf16[1536,1536]{1,0:T(8,128)(2,1)} %weight.1, ...), custom_call_target="tpu_custom_call" | custom-call | tf_op jit(solution)/shard_map/pallas_call | solution.py:812
  114.5 0.0 copy-start.4
  114.5 0.7 copy.16
  115.2 0.7 copy.17
  116.0 0.0 copy-done.4
  116.0 1.1 copy.18
  117.2 0.7 copy.19
Async XLA Ops:
  0.6 1.0 copy-start
  1.6 0.9 copy-start.1
  2.6 0.9 copy-start.2
  3.5 0.8 copy-start.3
  114.5 1.6 %copy-start.4 = (f32[2,128,1536]{2,1,0:T(8,128)S(1)}, f32[2,128,1536]{2,1,0:T(8,128)}, u32[]{:S(2)}) copy-start(f32[2,128,1536]{2,1,0:T(8,128)} %get-tuple-element.18) | copy-start | bytes 4718596

commit v2 on v1

--- a/solution.py
+++ b/solution.py
@@ -190,18 +190,19 @@
 
 
 def kernel(
-    values, queries, out_grad, weight, filt, m_fwd, m_inv, twist,
+    h_values, h_queries, h_out_grad, h_weight, h_filt, h_fwd, h_inv, h_twist,
     o_query, o_value, o_filter, o_weight,
-    w_in, og_x, g_gated, qt, val_t, gm_t, fil_t,
+    values, queries, out_grad, w_in, filt, m_fwd, m_inv, twist,
+    g_gated, qt, val_t, gm_t, fil_t,
     r1v, r1g, f1, xv, xg, hx, hrev, hs, lhi, llo, spec_v, spec_g, back,
     ymix, ygv, r2m, r2v, mix_t, gv_t, gp, gpx, gs, gr, gfi,
-    gat, gat_x, wa, ra0, ra1, sb0, sb1, rb0, rb1, sc, rc, sd, rd,
-    s_w, s_ogs, s_ogr, s_gts, s_gtr, s_gps, s_gpr,
+    gat, og_all, gat_all, wb, ry, sc, rc, sd, rd,
+    s_in, s_ogs, s_ogr, s_gas, s_gar, s_gxs, s_gps, s_gpr,
     s1vs, s1vr, s1gs, s1gr, s1fs, s1fr,
     s2vs, s2vr, s2gs, s2gr, s2fs, s2fr, s3fs, s3fr,
     sams, samr, savs, savr, sbms, sbmr, sbvs, sbvr,
     sags, sagr, sbgs, sbgr,
-    sras, srar, srbs, srbr, srcs, srcr, srds, srdr,
+    srys, sryr, srcs, srcr, srds, srdr,
 ):
     n = lax.axis_index("dp")
     ctx = lax.axis_index("ctx")
@@ -236,32 +237,46 @@
     def rounds(lo, hi, body):
         lax.fori_loop(lo, hi, lambda i, carry: (body(i), carry)[1], 0)
 
+    def place(i):
+        return lax.rem(y + lax.div(i, 4), 4) * 4 + lax.rem(x + lax.rem(i, 4), 4)
+
     def over_p(send):
-        rounds(1, 16, lambda i: send(lax.rem(p + i, 16)))
-
-    weight_copy = pltpu.make_async_copy(weight, w_in, s_w)
-    weight_copy.start()
+        rounds(1, 16, lambda i: send(place(i)))
+
+    inputs = [
+        pltpu.make_async_copy(src, dst, s_in.at[i])
+        for i, (src, dst) in enumerate(
+            [
+                (h_values, values), (h_queries, queries), (h_out_grad, out_grad),
+                (h_weight, w_in), (h_filt, filt), (h_fwd, m_fwd), (h_inv, m_inv),
+                (h_twist, twist),
+            ]
+        )
+    ]
+    for copy in inputs:
+        copy.start()
 
     barrier = pltpu.get_barrier_semaphore()
 
-    def greet_p(q):
-        pl.semaphore_signal(barrier, inc=1, device_id=at(q, z, c), device_id_type=MESH)
-
-    over_p(greet_p)
-
-    def greet_z(i):
-        zz = lax.rem(z + lax.div(i, 2), 8)
-        cc = lax.rem(c + lax.rem(i, 2), 2)
-        pl.semaphore_signal(barrier, inc=1, device_id=at(p, zz, cc), device_id_type=MESH)
-
-    rounds(1, 16, greet_z)
+    def greet(dev):
+        pl.semaphore_signal(barrier, inc=1, device_id=dev, device_id_type=MESH)
+
+    over_p(lambda q: greet(at(q, z, c)))
+    rounds(
+        1, 16,
+        lambda i: greet(
+            at(p, lax.rem(z + lax.div(i, 2), 8), lax.rem(c + lax.rem(i, 2), 2))
+        ),
+    )
+    rounds(1, 4, lambda i: greet(at(y * 4 + lax.rem(x + i, 4), z, 1 - c)))
 
     def turn_in(src, dst):
         for j in range(D // 128):
             dst[j * 128 : (j + 1) * 128, :] = src[:, j * 128 : (j + 1) * 128].T
 
+    inputs[0].wait()
     turn_in(values, val_t)
-    pl.semaphore_wait(barrier, 30)
+    pl.semaphore_wait(barrier, 33)
 
     def hop1(src, dst, ss, rs):
         local(src.at[pl.ds(p * 96, 96)], dst.at[p], rs.at[p])
@@ -276,12 +291,20 @@
 
     hop1(val_t, r1v, s1vs, s1vr)
 
-    other = at(p, z, 1 - c)
-    lanes_other = pl.ds(pl.multiple_of((1 - c) * 768, 768), 768)
-    lanes_own = pl.ds(pl.multiple_of(c * 768, 768), 768)
-    og_copy = remote(out_grad.at[:, lanes_other], og_x, s_ogs, s_ogr, other)
-    og_copy.start()
-
+    inputs[1].wait()
+    turn_in(queries, qt)
+    inputs[2].wait()
+    inputs[3].wait()
+
+    def gated_rows(i):
+        rows = pl.ds(pl.multiple_of(i * 256, 256), 256)
+        g = dot_t(w_in[rows, :], out_grad[...])
+        g_gated[rows, :] = g
+        gm_t[rows, :] = (g * qt[rows, :].astype(F32)).astype(BF16)
+
+    rounds(0, 6, gated_rows)
+
+    inputs[4].wait()
     for part in range(2):
         turn_in(filt.at[part], fil_t.at[part])
     two = jnp.logical_or(n == 0, n == 3)
@@ -306,35 +329,42 @@
 
     filter_hop1(0)
     pl.when(two)(lambda: filter_hop1(1))
+    hop1(gm_t, r1g, s1gs, s1gr)
+
+    core = lax.div(n, 2)
+
+    def z_of(u):
+        return u + (u >= 2).astype(jnp.int32) + (u >= 5).astype(jnp.int32)
 
     def hop2(r1, r1_sem, dst, ss, rs):
-        rounds(0, 16, lambda q: landed(r1.at[q], r1_sem.at[q]))
-        core = lax.div(n, 2)
-        slot = dst.at[lax.rem(n, 2), hc]
-
-        def send(i):
-            u = lax.rem(unit + i, 6)
-            zz = u + (u >= 2).astype(jnp.int32) + (u >= 5).astype(jnp.int32)
-            src = r1.at[:, pl.ds(u * 16, 16), :]
-            mine = jnp.logical_and(zz == z, core == c)
+        def row(j):
+            yy = lax.rem(y + j, 4)
+            blocks = pl.ds(yy * 4, 4)
+            rounds(0, 4, lambda q: landed(r1.at[yy * 4 + q], r1_sem.at[yy * 4 + q]))
+            slot = dst.at[lax.rem(n, 2), hc, blocks]
             sem = rs.at[lax.rem(n, 2), hc]
 
-            @pl.when(mine)
-            def _():
-                local(src, slot, sem)
-
-            @pl.when(jnp.logical_not(mine))
-            def _():
-                remote(src, slot, ss.at[u], sem, at(p, zz, core)).start()
-
-        rounds(0, 6, send)
+            def send(i):
+                u = lax.rem(unit + i, 6)
+                zz = z_of(u)
+                src = r1.at[blocks, pl.ds(u * 16, 16), :]
+                mine = jnp.logical_and(zz == z, core == c)
+
+                @pl.when(mine)
+                def _():
+                    local(src, slot, sem)
+
+                @pl.when(jnp.logical_not(mine))
+                def _():
+                    remote(src, slot, ss.at[u], sem, at(p, zz, core)).start()
+
+            rounds(0, 6, send)
+
+        rounds(0, 4, row)
 
     def hop2_done(r1, ss):
-        core = lax.div(n, 2)
-
         def done(u):
-            zz = u + (u >= 2).astype(jnp.int32) + (u >= 5).astype(jnp.int32)
-            mine = jnp.logical_and(zz == z, core == c)
+            mine = jnp.logical_and(z_of(u) == z, core == c)
 
             @pl.when(jnp.logical_not(mine))
             def _():
@@ -363,67 +393,65 @@
 
     filter_hop2(0)
     pl.when(two)(lambda: filter_hop2(1))
-
-    turn_in(queries, qt)
-    weight_copy.wait()
-
-    def gated_rows(i):
-        rows = pl.ds(pl.multiple_of(i * 256, 256), 256)
-        g = dot_t(w_in[rows, :], out_grad[...])
-        g_gated[rows, :] = g
-        gm_t[rows, :] = (g * qt[rows, :].astype(F32)).astype(BF16)
-
-    rounds(0, 6, gated_rows)
-    hop1(gm_t, r1g, s1gs, s1gr)
-
-    def transform(src, spec):
-        def one(nn):
-            def get(hh, cc, yy, xx):
-                return src[nn, 2 * hh + cc, 4 * yy + xx].astype(F32)
-
-            def put(s, v):
-                co, si = twist[0, s : s + 1, :], twist[1, s : s + 1, :]
-                re, im = v
-                if im is None:
-                    out = (re * co, -(re * si))
-                else:
-                    out = (re * co + im * si, im * co - re * si)
-                for j in range(2):
-                    hi, lo = split(out[j])
-                    lhi[s * 16 : s * 16 + 16, j * 128 : j * 128 + 128] = hi
-                    llo[s * 16 : s * 16 + 16, j * 128 : j * 128 + 128] = lo
-
-            blocks_forward(get, put)
-            spec[nn] = dot3(lhi[...], llo[...], m_fwd)
-
-        rounds(0, 2, one)
-
-    def untransform(product, dst):
-        def one(nn):
-            re, im = product(nn)
-            for j, v in enumerate((re, im)):
-                hi, lo = split(v)
-                lhi[:, j * 128 : j * 128 + 128] = hi
-                llo[:, j * 128 : j * 128 + 128] = lo
-            back[...] = dot3(lhi[...], llo[...], m_inv)
-
-            def get(s):
-                co = twist[0, s : s + 1, :] * (1.0 / SEQ)
-                si = twist[1, s : s + 1, :] * (1.0 / SEQ)
-                re = back[s * 16 : s * 16 + 16, :128]
-                im = back[s * 16 : s * 16 + 16, 128:]
-                return (re * co - im * si, im * co + re * si)
-
-            def put(hh, cc, yy, xx, v):
-                dst[nn, 2 * hh + cc, 4 * yy + xx] = v.astype(BF16)
-
-            blocks_inverse(get, put)
-
-        rounds(0, 2, one)
-
-    def hop_a(src, dst, ss, rs):
-        def send(i):
-            nn, hh, cc = lax.div(i, 4), lax.rem(lax.div(i, 2), 2), lax.rem(i, 2)
+    hop2(r1g, s1gr, xg, s2gs, s2gr)
+
+    other = at(p, z, 1 - c)
+
+    def og_send(i):
+        xx, cc = lax.rem(x + lax.div(i, 2), 4), lax.rem(c + lax.rem(i, 2), 2)
+        half = pl.ds(pl.multiple_of(cc * 768, 768), 768)
+        slot = og_all.at[x, pl.ds(pl.multiple_of(c * 128, 128), 128)]
+        remote(
+            out_grad.at[:, half], slot, s_ogs.at[i], s_ogr.at[x, c], at(y * 4 + xx, z, cc)
+        ).start()
+
+    own_half = pl.ds(pl.multiple_of(c * 768, 768), 768)
+    own_depth = pl.ds(pl.multiple_of(c * 128, 128), 128)
+    local(out_grad.at[:, own_half], og_all.at[x, own_depth], s_ogr.at[x, c])
+    rounds(1, 8, og_send)
+
+    def transform(src, spec, nn):
+        def get(hh, cc, yy, xx):
+            return src[nn, 2 * hh + cc, 4 * yy + xx].astype(F32)
+
+        def put(s, v):
+            co, si = twist[0, s : s + 1, :], twist[1, s : s + 1, :]
+            re, im = v
+            if im is None:
+                out = (re * co, -(re * si))
+            else:
+                out = (re * co + im * si, im * co - re * si)
+            for j in range(2):
+                hi, lo = split(out[j])
+                lhi[s * 16 : s * 16 + 16, j * 128 : j * 128 + 128] = hi
+                llo[s * 16 : s * 16 + 16, j * 128 : j * 128 + 128] = lo
+
+        blocks_forward(get, put)
+        spec[nn] = dot3(lhi[...], llo[...], m_fwd)
+
+    def untransform(product, dst, nn):
+        for j, v in enumerate(product):
+            hi, lo = split(v)
+            lhi[:, j * 128 : j * 128 + 128] = hi
+            llo[:, j * 128 : j * 128 + 128] = lo
+        back[...] = dot3(lhi[...], llo[...], m_inv)
+
+        def get(s):
+            co = twist[0, s : s + 1, :] * (1.0 / SEQ)
+            si = twist[1, s : s + 1, :] * (1.0 / SEQ)
+            re = back[s * 16 : s * 16 + 16, :128]
+            im = back[s * 16 : s * 16 + 16, 128:]
+            return (re * co - im * si, im * co + re * si)
+
+        def put(hh, cc, yy, xx, v):
+            dst[nn, 2 * hh + cc, 4 * yy + xx] = v.astype(BF16)
+
+        blocks_inverse(get, put)
+
+    def hop_a(src, dst, ss, rs, nn):
+        def send(j):
+            i = nn * 4 + j
+            hh, cc = lax.rem(lax.div(i, 2), 2), lax.rem(i, 2)
             zz = hh * 4 + 2 * c + nn
             mine = jnp.logical_and(zz == z, cc == c)
 
@@ -437,7 +465,7 @@
                     src.at[nn, 2 * hh + cc], dst.at[unit], ss.at[i], rs.at[unit], at(p, zz, cc)
                 ).start()
 
-        rounds(0, 8, send)
+        rounds(0, 4, send)
 
     def hop_a_done(src, ss):
         def done(i):
@@ -452,11 +480,17 @@
         rounds(0, 8, done)
 
     def hop_b(r2, r2_sem, dst, ss, rs):
-        rounds(0, 6, lambda u: landed(r2.at[u], r2_sem.at[u]))
-        local(r2.at[:, p], dst.at[p], rs.at[p])
-        over_p(
-            lambda q: remote(r2.at[:, q], dst.at[p], ss.at[q], rs.at[p], at(q, z, c)).start()
-        )
+        def relay(i):
+            u = lax.rem(unit + i, 6)
+            landed(r2.at[u], r2_sem.at[u])
+            local(r2.at[u, p], dst.at[p, u], rs.at[p])
+            over_p(
+                lambda q: remote(
+                    r2.at[u, q], dst.at[p, u], ss.at[q], rs.at[p], at(q, z, c)
+                ).start()
+            )
+
+        rounds(0, 6, relay)
 
     def hop_b_done(r2, ss):
         over_p(lambda q: left(r2.at[:, q], ss.at[q]))
@@ -470,19 +504,14 @@
         == 127 - lax.broadcasted_iota(jnp.int32, (128, 128), 1)
     ).astype(F32).astype(BF16)
 
+    for copy in inputs[5:]:
+        copy.wait()
+
     @pl.when(active)
     def _():
         for hh in range(2):
             landed(hx.at[hh, c], s2fr.at[hh])
             remote(hx.at[hh, c], hx.at[hh, c], s3fs.at[hh], s3fr.at[hh], other).start()
-        rounds(0, 8, lambda i: landed(xv.at[lax.div(i, 4), lax.rem(i, 4)],
-                                      s2vr.at[lax.div(i, 4), lax.rem(i, 4)]))
-        transform(xv, spec_v)
-
-    hop2(r1g, s1gr, xg, s2gs, s2gr)
-
-    @pl.when(active)
-    def _():
         for hh in range(2):
             landed(hx.at[hh, 1 - c], s3fr.at[hh])
 
@@ -502,25 +531,25 @@
             hs[s * 16 : s * 16 + 16, :128] = v[0] + turned[s, :16]
             hs[s * 16 : s * 16 + 16, 128:] = v[1] - turned[s, 16:]
 
-        def mixed_product(nn):
+        def values_part(nn):
+            rounds(0, 4, lambda i: landed(xv.at[nn, i], s2vr.at[nn, i]))
+            transform(xv, spec_v, nn)
             hr, hi = hs[:, :128], hs[:, 128:]
             vr, vi = spec_v[nn, :, :128], spec_v[nn, :, 128:]
-            return hr * vr - hi * vi, hr * vi + hi * vr
-
-        untransform(mixed_product, ymix)
-        hop_a(ymix, r2m, sams, samr)
-        rounds(0, 8, lambda i: landed(xg.at[lax.div(i, 4), lax.rem(i, 4)],
-                                      s2gr.at[lax.div(i, 4), lax.rem(i, 4)]))
-        transform(xg, spec_g)
-
-        def value_product(nn):
+            untransform((hr * vr - hi * vi, hr * vi + hi * vr), ymix, nn)
+            hop_a(ymix, r2m, sams, samr, nn)
+
+        rounds(0, 2, values_part)
+
+        def grads_part(nn):
+            rounds(0, 4, lambda i: landed(xg.at[nn, i], s2gr.at[nn, i]))
+            transform(xg, spec_g, nn)
             hr, hi = hs[:, :128], hs[:, 128:]
             gr_, gi = spec_g[nn, :, :128], spec_g[nn, :, 128:]
-            return gr_ * hr + gi * hi, gi * hr - gr_ * hi
-
-        untransform(value_product, ygv)
-        hop_a(ygv, r2v, savs, savr)
-
+            untransform((gr_ * hr + gi * hi, gi * hr - gr_ * hi), ygv, nn)
+            hop_a(ygv, r2v, savs, savr, nn)
+
+        rounds(0, 2, grads_part)
         re, im = 0.0, 0.0
         for nn in range(2):
             vr, vi = spec_v[nn, :, :128], spec_v[nn, :, 128:]
@@ -560,37 +589,17 @@
 
     rounds(0, 16, lambda q: landed(mix_t.at[q], sbmr.at[q]))
     mixed = mix_t[...].reshape(D, TOK).astype(F32)
-    gat[...] = (qt[...].astype(F32) * mixed).astype(BF16)
-    gat_copy = remote(gat, gat_x, s_gts, s_gtr, other)
-    gat_copy.start()
-    gq = (g_gated[...] * mixed).astype(BF16)
-    o_query[...] = dot_t(ident, gq).astype(BF16)
-
-    og_copy.wait_recv()
-    gat_copy.wait_recv()
-
-    def weight_rows(i):
-        yy, hh = lax.div(i, 2), lax.rem(i, 2)
-        rows = pl.ds(pl.multiple_of(i * 192, 192), 192)
-        w = dot(gat[rows, :], out_grad[:, lanes_own]) + dot(gat_x[rows, :], og_x[...])
-        for part in range(2):
-            wa[part, yy, hh] = (
-                w[:, part * 384 : (part + 1) * 384].astype(BF16).reshape(4, 48, 384)
-            )
-
-    rounds(0, 8, weight_rows)
-
-    def ra_send(i):
-        xx, yy = lax.rem(x + i, 4), lax.rem(y + i, 4)
-        remote(wa.at[0, :, :, xx], ra0.at[x], sras.at[0, i], srar.at[0, x],
-               at(y * 4 + xx, z, c)).start()
-        remote(wa.at[1, yy], ra1.at[y], sras.at[1, i], srar.at[1, y],
-               at(yy * 4 + x, z, c)).start()
-
-    rounds(1, 4, ra_send)
-
-    hop_b(r2v, savr, gv_t, sbvs, sbvr)
-
+    gat[...] = (qt[...].astype(F32) * mixed).astype(BF16).reshape(8, 4, 48, TOK)
+
+    def gat_send(i):
+        xx = lax.rem(x + i, 4)
+        remote(
+            gat.at[:, xx], gat_all.at[x, :, :, own_depth], s_gas.at[i], s_gar.at[x, c],
+            at(y * 4 + xx, z, c),
+        ).start()
+
+    rounds(1, 4, gat_send)
+    local(gat.at[:, x], gat_all.at[x, :, :, own_depth], s_gar.at[x, c])
     @pl.when(active)
     def _():
         rounds(0, 16, lambda q: landed(gr.at[q], sagr.at[q]))
@@ -610,44 +619,45 @@
 
         rounds(0, 8, send)
 
-    def ra_wait(i):
-        xx, yy = lax.rem(x + i, 4), lax.rem(y + i, 4)
-        landed(ra0.at[xx], srar.at[0, xx])
-        landed(ra1.at[yy], srar.at[1, yy])
-
-    rounds(1, 4, ra_wait)
-    sum0 = wa[0, :, :, x].astype(F32)
-    sum1 = wa[1, y].astype(F32)
+    gq = (g_gated[...] * mixed).astype(BF16)
+    o_query[...] = dot_t(ident, gq).astype(BF16)
+
+    def gat_pass(i):
+        xx = lax.rem(x + i, 4)
+        here = gat_all.at[xx, :, :, own_depth]
+        landed(here, s_gar.at[xx, c])
+        remote(here, here, s_gxs.at[xx], s_gar.at[xx, c], other).start()
+
+    rounds(0, 4, gat_pass)
+
+    other_depth = pl.ds(pl.multiple_of((1 - c) * 128, 128), 128)
+
+    def w_wait(xx):
+        landed(gat_all.at[xx, :, :, other_depth], s_gar.at[xx, 1 - c])
+        landed(og_all.at[xx, own_depth], s_ogr.at[xx, c])
+        landed(og_all.at[xx, other_depth], s_ogr.at[xx, 1 - c])
+
+    rounds(0, 4, w_wait)
+
+    def weight_rows(i):
+        yy = lax.rem(y + i, 4)
+        total = dot(gat_all[0, pl.ds(yy * 2, 2)].reshape(96, 256), og_all[0])
+        for xx in range(1, 4):
+            total = total + dot(gat_all[xx, pl.ds(yy * 2, 2)].reshape(96, 256), og_all[xx])
+        wb[yy] = total.astype(BF16).reshape(2, 48, 768)
+
+        @pl.when(i < 4)
+        def _():
+            remote(wb.at[yy], ry.at[y], srys.at[i], sryr.at[y], at(yy * 4 + x, z, c)).start()
+
+    rounds(1, 5, weight_rows)
+    hop_b(r2v, savr, gv_t, sbvs, sbvr)
+
+    rounds(1, 4, lambda i: landed(ry.at[lax.rem(y + i, 4)], sryr.at[lax.rem(y + i, 4)]))
+    total = wb[y].astype(F32)
     for i in range(1, 4):
-        sum0 = sum0 + ra0[lax.rem(x + i, 4)].astype(F32)
-        sum1 = sum1 + ra1[lax.rem(y + i, 4)].astype(F32)
-    sb0[...] = sum0.astype(BF16)
-    sb1[...] = sum1.astype(BF16)
-
-    def rb_send(i):
-        xx, yy = lax.rem(x + i, 4), lax.rem(y + i, 4)
-        remote(sb0.at[yy], rb0.at[y], srbs.at[0, i], srbr.at[0, y], at(yy * 4 + x, z, c)).start()
-        remote(sb1.at[:, xx], rb1.at[x], srbs.at[1, i], srbr.at[1, x],
-               at(y * 4 + xx, z, c)).start()
-
-    rounds(1, 4, rb_send)
-
-    rounds(0, 16, lambda q: landed(gv_t.at[q], sbvr.at[q]))
-    o_value[...] = dot_t(ident, gv_t[...].reshape(D, TOK)).astype(BF16)
-
-    def rb_wait(i):
-        xx, yy = lax.rem(x + i, 4), lax.rem(y + i, 4)
-        landed(rb0.at[yy], srbr.at[0, yy])
-        landed(rb1.at[xx], srbr.at[1, xx])
-
-    rounds(1, 4, rb_wait)
-    sum0 = sb0[y].astype(F32)
-    sum1 = sb1[:, x].astype(F32)
-    for i in range(1, 4):
-        sum0 = sum0 + rb0[lax.rem(y + i, 4)].astype(F32)
-        sum1 = sum1 + rb1[lax.rem(x + i, 4)].astype(F32)
-    sc[:, :, :, :384] = sum0.astype(BF16).reshape(2, 3, 16, 384)
-    sc[:, :, :, 384:] = sum1.astype(BF16).reshape(2, 3, 16, 384)
+        total = total + ry[lax.rem(y + i, 4)].astype(F32)
+    sc[...] = total.astype(BF16).reshape(2, 3, 16, 768)
 
     def rc_send(i):
         hh, t = lax.div(i, 3), lax.rem(i, 3)
@@ -662,6 +672,9 @@
             remote(sc.at[hh, t], rc.at[z], srcs.at[i], srcr.at[z], at(p, zz, c)).start()
 
     rounds(0, 6, rc_send)
+
+    rounds(0, 16, lambda q: landed(gv_t.at[q], sbvr.at[q]))
+    o_value[...] = dot_t(ident, gv_t[...].reshape(D, TOK)).astype(BF16)
     owner = n < 3
 
     @pl.when(owner)
@@ -687,10 +700,7 @@
 
         rounds(0, 8, send)
 
-    def gf_wait(u):
-        landed(gfi.at[:, u], sbgr.at[u])
-
-    rounds(0, 6, gf_wait)
+    rounds(0, 6, lambda u: landed(gfi.at[:, u], sbgr.at[u]))
     straight = jnp.logical_or(
         lax.rem(ctx, 4) == 1, jnp.logical_and(c == 0, ctx <= 32)
     )
@@ -718,8 +728,6 @@
 
     hop1_done(val_t, s1vs)
     hop1_done(gm_t, s1gs)
-    og_copy.wait_send()
-    gat_copy.wait_send()
     over_p(lambda q: left(f_src(0, q), s1fs.at[0, q]))
     filter_hop2_done(0)
 
@@ -732,6 +740,9 @@
     hop2_done(r1g, s2gs)
     hop_b_done(r2m, sbms)
     hop_b_done(r2v, sbvs)
+    rounds(1, 8, lambda i: left(og_all.at[x, own_depth], s_ogs.at[i]))
+    rounds(1, 4, lambda i: left(gat.at[:, x], s_gas.at[i]))
+    rounds(0, 4, lambda i: left(gat_all.at[i, :, :, own_depth], s_gxs.at[i]))
 
     @pl.when(active)
     def _():
@@ -749,13 +760,7 @@
 
         rounds(0, 8, done)
 
-    def ra_done(i):
-        left(ra0.at[0], sras.at[0, i])
-        left(ra1.at[0], sras.at[1, i])
-        left(rb0.at[0], srbs.at[0, i])
-        left(rb1.at[0], srbs.at[1, i])
-
-    rounds(1, 4, ra_done)
+    rounds(1, 4, lambda i: left(wb.at[0], srys.at[i]))
 
     def rc_done(i):
         @pl.when(lax.div(i, 3) * 4 + lax.rem(i, 3) != z)
@@ -785,8 +790,9 @@
         return pltpu.VMEM(shape, dtype)
 
     scratch = [
-        held(D, D), held(TOK, 768), held(D, TOK, dtype=F32), held(D, TOK),
-        held(D, TOK), held(D, TOK), held(2, D, TOK),
+        held(TOK, D), held(TOK, D), held(TOK, D), held(D, D), held(2, TOK, D),
+        held(2, 256, 256), held(2, 256, 256), held(2, 40, TOK, dtype=F32),
+        held(D, TOK, dtype=F32), held(D, TOK), held(D, TOK), held(D, TOK), held(2, D, TOK),
         held(16, 96, TOK), held(16, 96, TOK), held(2, 16, 2, 16, TOK),
         held(2, 4, 16, 16, TOK), held(2, 4, 16, 16, TOK), held(2, 2, 16, 2, 16, TOK),
         held(SLOTS * 32, TOK), held(ROWS, 256, dtype=F32),
@@ -797,17 +803,15 @@
         held(16, 6, 16, TOK), held(16, 6, 16, TOK),
         held(ROWS, 256, dtype=F32), held(272, 256, dtype=F32),
         held(16, 2, 2, 16, TOK), held(16, 2, 2, 16, TOK), held(16, 6, 2, 16, TOK),
-        held(D, TOK), held(D, TOK),
-        held(2, 4, 2, 4, 48, 384), held(4, 4, 2, 48, 384), held(4, 2, 4, 48, 384),
-        held(4, 2, 48, 384), held(2, 4, 48, 384), held(4, 2, 48, 384), held(4, 2, 48, 384),
+        held(8, 4, 48, TOK), held(4, 256, 768), held(4, 8, 48, 256),
+        held(4, 2, 48, 768), held(4, 2, 48, 768),
         held(2, 3, 16, 768), held(8, 16, 768), held(16, 768), held(3, 2, 16, 768),
-        dma, dma, dma, dma, dma, dma, dma,
+        dma((8,)), dma((8,)), dma((4, 2)), dma((4,)), dma((4, 2)), dma((4,)), dma, dma,
         dma((16,)), dma((16,)), dma((16,)), dma((16,)), dma((2, 16)), dma((2, 16)),
         dma((6,)), dma((2, 4)), dma((6,)), dma((2, 4)), dma((2,)), dma((2,)), dma((2,)), dma((2,)),
         dma((8,)), dma((6,)), dma((8,)), dma((6,)), dma((16,)), dma((16,)), dma((16,)), dma((16,)),
         dma((16,)), dma((16,)), dma((8,)), dma((6,)),
-        dma((2, 4)), dma((2, 4)), dma((2, 4)), dma((2, 4)), dma((6,)), dma((8,)),
-        dma((8,)), dma((3, 2)),
+        dma((4,)), dma((4,)), dma((6,)), dma((8,)), dma((8,)), dma((3, 2)),
     ]
     grad_query, grad_value, grad_filter, grad_weight = pl.pallas_call(
         kernel,
@@ -817,11 +821,11 @@
             jax.ShapeDtypeStruct((2, TOK, D), F32),
             jax.ShapeDtypeStruct((24, D), F32),
         ),
-        in_specs=[vmem, vmem, vmem, pl.BlockSpec(memory_space=pl.ANY)] + [vmem] * 4,
+        in_specs=[pl.BlockSpec(memory_space=pl.ANY)] * 8,
         out_specs=(vmem,) * 4,
         scratch_shapes=scratch,
         compiler_params=pltpu.CompilerParams(
-            collective_id=0, has_side_effects=True, vmem_limit_bytes=52 * 2**20
+            collective_id=0, has_side_effects=True, vmem_limit_bytes=60 * 2**20
         ),
     )(values[0], queries[0], out_grad[0], out_weight, filter_spec,
       jnp.asarray(m_fwd), jnp.asarray(m_inv), jnp.asarray(twist))

time: 118 us -> 104 us (0.88)
  Pallas kernels: 110 us -> 97.4 us
  local copies, waits for them, and re-layouts: 7.01 us -> 5.46 us
    pallas_call x1, Pallas kernels: 110 us -> 97.4 us  [on_device(): pl.pallas_call(kernel, out_shape=(jax.ShapeDtypeStruct((TOK, D), BF16), j...]
    unnamed x14 -> x8, local copies, waits for them, and re-layouts: 7.01 us -> 5.46 us
where the time goes in v2:
time: 104 us
  Pallas kernels  97.4 us (94%)
  local copies, waits for them, and re-layouts  5.46 us (5%)
    pallas_call x1, Pallas kernels, on_device(): pl.pallas_call(kernel, out_shape=(jax.ShapeDtypeStruct((TOK, D), BF16), j...  97.4 us
    unnamed x8, local copies, waits for them, and re-layouts  5.46 us

profile of v2, /device:TPU:1, one launch (start us, length us, event | category | flops | bytes accessed | tf_op | source)
XLA Modules:
  0.0 103.5 jit_solution(11477197700026888695)
XLA Ops:
  0.6 97.4 %shard_map.111 = (bf16[128,1536]{1,0:T(8,128)(2,1)}, bf16[128,1536]{1,0:T(8,128)(2,1)}, f32[2,128,1536]{2,1,0:T(8,128)}, f32[24,1536]{1,0:T(8,128)}) custom-call(bf16[128,1536]{1,0:T(8,128)(2,1)} %bitcast.5, bf16[128,1536]{1,0:T(8,128)(2,1)} %bitcast.6, bf16[128,1536]{1,0:T(8,128)(2,1)} %bitcast.7, bf16[1536,1536]{1,0:T(8,128)(2,1)} %h_weight.1, ...), custom_call_target="tpu_custom_call" | custom-call | tf_op jit(solution)/shard_map/pallas_call | solution.py:816
  98.0 0.0 copy-start
  98.0 1.9 %copy.16 = bf16[1,128,1536]{2,1,0:T(8,128)(2,1)} copy(bf16[1,128,1536]{2,1,0:T(8,128)(2,1)} %bitcast.9) | data formatting | bytes 786432
  99.9 1.8 %copy.17 = bf16[1,128,1536]{2,1,0:T(8,128)(2,1)} copy(bf16[1,128,1536]{2,1,0:T(8,128)(2,1)} %bitcast.8) | data formatting | bytes 786432
  101.7 0.0 copy-done
  101.7 0.0 copy-start.1
  101.7 1.1 %copy.18 = f32[2,128,1536]{2,1,0:T(8,128)} copy(f32[2,128,1536]{2,1,0:T(8,128)S(1)} %copy-done) | data formatting | bytes 3145728
  102.8 0.0 copy-done.1
  102.9 0.7 copy.19
Async XLA Ops:
  98.0 3.7 %copy-start = (f32[2,128,1536]{2,1,0:T(8,128)S(1)}, f32[2,128,1536]{2,1,0:T(8,128)}, u32[]{:S(2)}) copy-start(f32[2,128,1536]{2,1,0:T(8,128)} %get-tuple-element.18) | copy-start | bytes 4718596
  101.7 1.1 %copy-start.1 = (f32[24,1536]{1,0:T(8,128)S(1)}, f32[24,1536]{1,0:T(8,128)}, u32[]{:S(2)}) copy-start(f32[24,1536]{1,0:T(8,128)} %get-tuple-element.19) | copy-start | bytes 442372

commit v3 on v2

--- a/solution.py
+++ b/solution.py
@@ -191,13 +191,13 @@
 
 def kernel(
     h_values, h_queries, h_out_grad, h_weight, h_filt, h_fwd, h_inv, h_twist,
-    o_query, o_value, o_filter, o_weight,
+    o_query, o_value, o_gf, o_rd,
     values, queries, out_grad, w_in, filt, m_fwd, m_inv, twist,
     g_gated, qt, val_t, gm_t, fil_t,
     r1v, r1g, f1, xv, xg, hx, hrev, hs, lhi, llo, spec_v, spec_g, back,
     ymix, ygv, r2m, r2v, mix_t, gv_t, gp, gpx, gs, gr, gfi,
-    gat, og_all, gat_all, wb, ry, sc, rc, sd, rd,
-    s_in, s_ogs, s_ogr, s_gas, s_gar, s_gxs, s_gps, s_gpr,
+    k_query, k_value, s_out, s_gfo, qx, mx, og_all, gat_all, wb, ry, sc, rc, sd, rd,
+    s_in, s_ogs, s_ogr, s_qxs, s_qxr, s_mxs, s_mxr, s_gxr, s_gxs, s_gps, s_gpr,
     s1vs, s1vr, s1gs, s1gr, s1fs, s1fr,
     s2vs, s2vr, s2gs, s2gr, s2fs, s2fr, s3fs, s3fr,
     sams, samr, savs, savr, sbms, sbmr, sbvs, sbvr,
@@ -292,7 +292,13 @@
     hop1(val_t, r1v, s1vs, s1vr)
 
     inputs[1].wait()
-    turn_in(queries, qt)
+    for j in range(D // 128):
+        piece = queries[:, j * 128 : (j + 1) * 128].T
+        for g in range(8):
+            k = j * 8 + g
+            qt[k // 12, (k // 3) % 4, (k % 3) * 16 : (k % 3) * 16 + 16, :] = (
+                piece[g * 16 : g * 16 + 16]
+            )
     inputs[2].wait()
     inputs[3].wait()
 
@@ -300,9 +306,9 @@
         rows = pl.ds(pl.multiple_of(i * 256, 256), 256)
         g = dot_t(w_in[rows, :], out_grad[...])
         g_gated[rows, :] = g
-        gm_t[rows, :] = (g * qt[rows, :].astype(F32)).astype(BF16)
 
     rounds(0, 6, gated_rows)
+    gm_t[...] = (g_gated[...] * qt[...].reshape(D, TOK).astype(F32)).astype(BF16)
 
     inputs[4].wait()
     for part in range(2):
@@ -404,6 +410,15 @@
         remote(
             out_grad.at[:, half], slot, s_ogs.at[i], s_ogr.at[x, c], at(y * 4 + xx, z, cc)
         ).start()
+
+    def qx_send(i):
+        xx = lax.rem(x + i, 4)
+        remote(
+            qt.at[:, xx], qx.at[x], s_qxs.at[i], s_qxr.at[x], at(y * 4 + xx, z, c)
+        ).start()
+
+    rounds(1, 4, qx_send)
+    local(qt.at[:, x], qx.at[x], s_qxr.at[x])
 
     own_half = pl.ds(pl.multiple_of(c * 768, 768), 768)
     own_depth = pl.ds(pl.multiple_of(c * 128, 128), 128)
@@ -482,7 +497,8 @@
     def hop_b(r2, r2_sem, dst, ss, rs):
         def relay(i):
             u = lax.rem(unit + i, 6)
-            landed(r2.at[u], r2_sem.at[u])
+            if r2_sem is not None:
+                landed(r2.at[u], r2_sem.at[u])
             local(r2.at[u, p], dst.at[p, u], rs.at[p])
             over_p(
                 lambda q: remote(
@@ -561,7 +577,58 @@
         gp_rows = pl.ds(pl.multiple_of((1 - c) * 256, 256), 272)
         remote(gp.at[gp_rows], gpx, s_gps, s_gpr, other).start()
 
-    hop_b(r2m, samr, mix_t, sbms, sbmr)
+    def mixed_share(i):
+        u = lax.rem(unit + i, 6)
+        landed(r2m.at[u], samr.at[u])
+        xx = 2 * lax.rem(x, 2) + lax.div(u, 3)
+        yh = y * 2 + lax.div(x, 2)
+        slot = mx.at[:, yh, pl.ds(pl.multiple_of(lax.rem(u, 3) * 16, 16), 16), :]
+
+        def send(j):
+            yy = lax.rem(y + j, 4)
+            src = r2m.at[u, pl.ds(yy * 4, 4)]
+            mine = jnp.logical_and(j == 0, xx == x)
+
+            @pl.when(mine)
+            def _():
+                local(src, slot, s_mxr.at[yh])
+
+            @pl.when(jnp.logical_not(mine))
+            def _():
+                remote(
+                    src, slot, s_mxs.at[u, yy], s_mxr.at[yh], at(yy * 4 + xx, z, c)
+                ).start()
+
+        rounds(0, 4, send)
+
+    def mixed_share_done(u):
+        xx = 2 * lax.rem(x, 2) + lax.div(u, 3)
+
+        def done(yy):
+            mine = jnp.logical_and(yy == y, xx == x)
+
+            @pl.when(jnp.logical_not(mine))
+            def _():
+                left(r2m.at[u, pl.ds(yy * 4, 4)], s_mxs.at[u, yy])
+
+        rounds(0, 4, done)
+
+    hop1_done(val_t, s1vs)
+    hop1_done(gm_t, s1gs)
+    over_p(lambda q: left(f_src(0, q), s1fs.at[0, q]))
+    filter_hop2_done(0)
+
+    @pl.when(two)
+    def _():
+        over_p(lambda q: left(f_src(1, q), s1fs.at[1, q]))
+        filter_hop2_done(1)
+
+    hop2_done(r1v, s2vs)
+    hop2_done(r1g, s2gs)
+    rounds(1, 8, lambda i: left(og_all.at[x, own_depth], s_ogs.at[i]))
+    rounds(1, 4, lambda i: left(qx.at[0], s_qxs.at[i]))
+
+    rounds(0, 6, mixed_share)
 
     @pl.when(active)
     def _():
@@ -587,53 +654,75 @@
             lambda q: remote(gs.at[q], gr.at[p], sags.at[q], sagr.at[p], at(q, z, c)).start()
         )
 
-    rounds(0, 16, lambda q: landed(mix_t.at[q], sbmr.at[q]))
-    mixed = mix_t[...].reshape(D, TOK).astype(F32)
-    gat[...] = (qt[...].astype(F32) * mixed).astype(BF16).reshape(8, 4, 48, TOK)
-
-    def gat_send(i):
+    rounds(0, 8, lambda i: landed(mx.at[:, i], s_mxr.at[i]))
+
+    def gate(i):
         xx = lax.rem(x + i, 4)
-        remote(
-            gat.at[:, xx], gat_all.at[x, :, :, own_depth], s_gas.at[i], s_gar.at[x, c],
-            at(y * 4 + xx, z, c),
-        ).start()
-
-    rounds(1, 4, gat_send)
-    local(gat.at[:, x], gat_all.at[x, :, :, own_depth], s_gar.at[x, c])
+        landed(qx.at[xx], s_qxr.at[xx])
+        gat_all[xx, :, :, own_depth] = (qx[xx].astype(F32) * mx[xx].astype(F32)).astype(BF16)
+        here = gat_all.at[xx, :, :, own_depth]
+        remote(here, here, s_gxs.at[xx], s_gxr.at[xx], other).start()
+
+    rounds(0, 4, gate)
+
     @pl.when(active)
     def _():
         rounds(0, 16, lambda q: landed(gr.at[q], sagr.at[q]))
-
-        def send(i):
-            hh, nn = lax.rem(i, 2), lax.rem(lax.div(i, 2) + n, 4)
-            zz = hh * 4 + nn
-            sem = sbgr.at[unit]
-
-            @pl.when(zz == z)
-            def _():
-                local(gr.at[:, hh], gfi.at[:, unit], sem)
-
-            @pl.when(zz != z)
-            def _():
-                remote(gr.at[:, hh], gfi.at[:, unit], sbgs.at[zz], sem, at(p, zz, c)).start()
-
-        rounds(0, 8, send)
-
-    gq = (g_gated[...] * mixed).astype(BF16)
-    o_query[...] = dot_t(ident, gq).astype(BF16)
-
-    def gat_pass(i):
-        xx = lax.rem(x + i, 4)
-        here = gat_all.at[xx, :, :, own_depth]
-        landed(here, s_gar.at[xx, c])
-        remote(here, here, s_gxs.at[xx], s_gar.at[xx, c], other).start()
-
-    rounds(0, 4, gat_pass)
+        local(gr.at[:, h], gfi.at[:, unit], sbgr.at[unit])
+        first = [
+            h * 4 + jnp.where(n == 0, 1, jnp.where(n == 1, 0, 2)),
+            h * 4 + jnp.where(n == 3, 1, 2),
+            (1 - h) * 4 + jnp.where(n == 0, 1, 0),
+            (1 - h) * 4 + jnp.where(n == 3, 2, 3),
+        ]
+        for k, zz in enumerate(first):
+            half = h if k < 2 else 1 - h
+            remote(
+                gr.at[:, half], gfi.at[:, unit], sbgs.at[k], sbgr.at[unit], at(p, zz, c)
+            ).start()
+
+    mate = h * 4 + n + 1 - 2 * lax.rem(n, 2)
+    passes = [
+        (h * 4 + 1, n == 2), (h * 4, n == 2), (h * 4 + 3, n == 1),
+        ((1 - h) * 4 + 3, jnp.logical_or(n == 0, n == 2)),
+        ((1 - h) * 4, jnp.logical_or(n == 1, n == 3)),
+        ((1 - h) * 4 + 1, jnp.logical_or(n == 0, n == 3)),
+    ]
+
+    def gf_pass(k):
+        source, here = passes[k]
+        u = unit_at(source)
+
+        @pl.when(here)
+        def _():
+            landed(gfi.at[:, u], sbgr.at[u])
+            remote(
+                gfi.at[:, u], gfi.at[:, u], sbgs.at[4 + k], sbgr.at[u], at(p, mate, c)
+            ).start()
+
+    def gf_last(k):
+        source, here = passes[k]
+        u = unit_at(source)
+
+        @pl.when(jnp.logical_not(here))
+        def _():
+            landed(gfi.at[:, u], sbgr.at[u])
+
+        pltpu.make_async_copy(gfi.at[:, u], o_gf.at[:, u], s_gfo.at[k]).start()
+
+    def gf_left(k):
+        source, here = passes[k]
+        u = unit_at(source)
+
+        @pl.when(here)
+        def _():
+            left(gfi.at[:, u], sbgs.at[4 + k])
+
 
     other_depth = pl.ds(pl.multiple_of((1 - c) * 128, 128), 128)
 
     def w_wait(xx):
-        landed(gat_all.at[xx, :, :, other_depth], s_gar.at[xx, 1 - c])
+        landed(gat_all.at[xx, :, :, other_depth], s_gxr.at[xx])
         landed(og_all.at[xx, own_depth], s_ogr.at[xx, c])
         landed(og_all.at[xx, other_depth], s_ogr.at[xx, 1 - c])
 
@@ -651,8 +740,8 @@
             remote(wb.at[yy], ry.at[y], srys.at[i], sryr.at[y], at(yy * 4 + x, z, c)).start()
 
     rounds(1, 5, weight_rows)
+    hop_b(r2m, None, mix_t, sbms, sbmr)
     hop_b(r2v, savr, gv_t, sbvs, sbvr)
-
     rounds(1, 4, lambda i: landed(ry.at[lax.rem(y + i, 4)], sryr.at[lax.rem(y + i, 4)]))
     total = wb[y].astype(F32)
     for i in range(1, 4):
@@ -672,76 +761,16 @@
             remote(sc.at[hh, t], rc.at[z], srcs.at[i], srcr.at[z], at(p, zz, c)).start()
 
     rounds(0, 6, rc_send)
-
-    rounds(0, 16, lambda q: landed(gv_t.at[q], sbvr.at[q]))
-    o_value[...] = dot_t(ident, gv_t[...].reshape(D, TOK)).astype(BF16)
-    owner = n < 3
-
-    @pl.when(owner)
-    def _():
-        rounds(0, 8, lambda i: landed(rc.at[i], srcr.at[i]))
-        total = rc[0].astype(F32)
-        for i in range(1, 8):
-            total = total + rc[i].astype(F32)
-        sd[...] = total.astype(BF16)
-
-        def send(i):
-            nn, cc = lax.div(i, 2), lax.rem(i, 2)
-            mine = jnp.logical_and(nn == n, cc == c)
-
-            @pl.when(mine)
-            def _():
-                local(sd, rd.at[n, c], srdr.at[n, c])
-
-            @pl.when(jnp.logical_not(mine))
-            def _():
-                remote(sd, rd.at[n, c], srds.at[i], srdr.at[n, c],
-                       at(p, h * 4 + nn, cc)).start()
-
-        rounds(0, 8, send)
-
-    rounds(0, 6, lambda u: landed(gfi.at[:, u], sbgr.at[u]))
-    straight = jnp.logical_or(
-        lax.rem(ctx, 4) == 1, jnp.logical_and(c == 0, ctx <= 32)
-    )
-    pick = jnp.where(straight, ident.astype(F32), flip.astype(F32)).astype(BF16)
-    sign = jnp.where(straight, 1.0, -1.0)
-    o_filter[0] = dot_t(pick, gfi[:, :, 0].reshape(D, TOK))
-    o_filter[1] = dot_t(pick, gfi[:, :, 1].reshape(D, TOK)) * sign
-
-    for t in range(3):
-        for cc in range(2):
-            landed(rd.at[t, cc], srdr.at[t, cc])
-    scale = 1.0 / math.sqrt(4 * SEQ)
-    for cc in range(2):
-        cols = slice(cc * 768, (cc + 1) * 768)
-
-        @pl.when(c == 0)
-        def _():
-            o_weight[0:16, cols] = rd[0, cc].astype(F32) * scale
-            o_weight[16:24, cols] = rd[1, cc].astype(F32)[0:8] * scale
-
-        @pl.when(c == 1)
-        def _():
-            o_weight[0:8, cols] = rd[1, cc].astype(F32)[8:16] * scale
-            o_weight[8:24, cols] = rd[2, cc].astype(F32) * scale
-
-    hop1_done(val_t, s1vs)
-    hop1_done(gm_t, s1gs)
-    over_p(lambda q: left(f_src(0, q), s1fs.at[0, q]))
-    filter_hop2_done(0)
-
-    @pl.when(two)
-    def _():
-        over_p(lambda q: left(f_src(1, q), s1fs.at[1, q]))
-        filter_hop2_done(1)
-
-    hop2_done(r1v, s2vs)
-    hop2_done(r1g, s2gs)
+    for k in range(6):
+        gf_pass(k)
+    rounds(0, 16, lambda q: landed(mix_t.at[q], sbmr.at[q]))
+    gq = (g_gated[...] * mix_t[...].reshape(D, TOK).astype(F32)).astype(BF16)
+    k_query[...] = dot_t(ident, gq).astype(BF16)
+    query_out = pltpu.make_async_copy(k_query, o_query, s_out.at[0])
+    query_out.start()
+
+    rounds(0, 6, mixed_share_done)
     hop_b_done(r2m, sbms)
-    hop_b_done(r2v, sbvs)
-    rounds(1, 8, lambda i: left(og_all.at[x, own_depth], s_ogs.at[i]))
-    rounds(1, 4, lambda i: left(gat.at[:, x], s_gas.at[i]))
     rounds(0, 4, lambda i: left(gat_all.at[i, :, :, own_depth], s_gxs.at[i]))
 
     @pl.when(active)
@@ -753,21 +782,63 @@
         left(gpx, s_gps)
         over_p(lambda q: left(gs.at[q], sags.at[q]))
 
-        def done(zz):
-            @pl.when(zz != z)
+    rounds(1, 4, lambda i: left(wb.at[0], srys.at[i]))
+    rounds(0, 16, lambda q: landed(gv_t.at[q], sbvr.at[q]))
+    k_value[...] = dot_t(ident, gv_t[...].reshape(D, TOK)).astype(BF16)
+    value_out = pltpu.make_async_copy(k_value, o_value, s_out.at[1])
+    value_out.start()
+    owner = n < 3
+
+    @pl.when(owner)
+    def _():
+        rounds(0, 8, lambda i: landed(rc.at[i], srcr.at[i]))
+        total = rc[0].astype(F32)
+        for i in range(1, 8):
+            total = total + rc[i].astype(F32)
+        sd[...] = total.astype(BF16)
+
+        def send(i):
+            nn, cc = lax.div(i, 2), lax.rem(i, 2)
+            mine = jnp.logical_and(nn == n, cc == c)
+
+            @pl.when(mine)
             def _():
-                left(gr.at[:, 0], sbgs.at[zz])
-
-        rounds(0, 8, done)
-
-    rounds(1, 4, lambda i: left(wb.at[0], srys.at[i]))
-
+                local(sd, rd.at[n, c], srdr.at[n, c])
+
+            @pl.when(jnp.logical_not(mine))
+            def _():
+                remote(sd, rd.at[n, c], srds.at[i], srdr.at[n, c],
+                       at(p, h * 4 + nn, cc)).start()
+
+        rounds(0, 8, send)
+
+    hop_b_done(r2v, sbvs)
     def rc_done(i):
         @pl.when(lax.div(i, 3) * 4 + lax.rem(i, 3) != z)
         def _():
             left(sd, srcs.at[i])
 
     rounds(0, 6, rc_done)
+
+    for k in range(6):
+        gf_last(k)
+    for t in range(3):
+        for cc in range(2):
+            landed(rd.at[t, cc], srdr.at[t, cc])
+    weight_out = pltpu.make_async_copy(rd, o_rd, s_out.at[3])
+    weight_out.start()
+
+    for copy in (query_out, value_out, weight_out):
+        copy.wait()
+    for k in range(6):
+        left(gfi.at[:, 0], s_gfo.at[k])
+
+    @pl.when(active)
+    def _():
+        rounds(0, 4, lambda k: left(gr.at[:, 0], sbgs.at[k]))
+
+    for k in range(6):
+        gf_left(k)
 
     @pl.when(owner)
     def _():
@@ -781,6 +852,56 @@
         rounds(0, 8, done)
 
 
+def finish(
+    h_query, h_value, h_gf, h_rd, o_query, o_value, o_filter, o_weight,
+    gfi, rd, k_query, k_value, k_filter, sem
+):
+    ctx = lax.axis_index("ctx")
+    c = lax.rem(ctx, 2)
+    gf_in = pltpu.make_async_copy(h_gf, gfi, sem.at[0])
+    rd_in = pltpu.make_async_copy(h_rd, rd, sem.at[1])
+    query_in = pltpu.make_async_copy(h_query, k_query, sem.at[2])
+    value_in = pltpu.make_async_copy(h_value, k_value, sem.at[3])
+    for copy in (gf_in, query_in, value_in, rd_in):
+        copy.start()
+    row = lax.broadcasted_iota(jnp.int32, (128, 128), 0)
+    col = lax.broadcasted_iota(jnp.int32, (128, 128), 1)
+    straight = jnp.logical_or(lax.rem(ctx, 4) == 1, jnp.logical_and(c == 0, ctx <= 32))
+    pick = (row == jnp.where(straight, col, 127 - col)).astype(F32).astype(BF16)
+    sign = jnp.where(straight, 1.0, -1.0)
+    outs = [
+        pltpu.make_async_copy(k_query, o_query, sem.at[6]),
+        pltpu.make_async_copy(k_value, o_value, sem.at[7]),
+    ]
+    gf_in.wait()
+    for copy, out in zip((query_in, value_in), outs):
+        copy.wait()
+        out.start()
+    for part in range(2):
+        value_part = dot_t(pick, gfi[:, :, part].reshape(D, TOK))
+        k_filter[part] = value_part if part == 0 else value_part * sign
+        out = pltpu.make_async_copy(k_filter.at[part], o_filter.at[part], sem.at[4 + part])
+        out.start()
+        outs.append(out)
+    rd_in.wait()
+    scale = 1.0 / math.sqrt(4 * SEQ)
+    for cc in range(2):
+        cols = slice(cc * 768, (cc + 1) * 768)
+
+        @pl.when(c == 0)
+        def _():
+            o_weight[0:16, cols] = rd[0, cc].astype(F32) * scale
+            o_weight[16:24, cols] = rd[1, cc].astype(F32)[0:8] * scale
+
+        @pl.when(c == 1)
+        def _():
+            o_weight[0:8, cols] = rd[1, cc].astype(F32)[8:16] * scale
+            o_weight[8:24, cols] = rd[2, cc].astype(F32) * scale
+
+    for copy in outs:
+        copy.wait()
+
+
 def on_device(queries, values, out_grad, out_weight, filter_spec):
     m_fwd, m_inv, twist = tables()
     vmem = pl.BlockSpec(memory_space=pltpu.VMEM)
@@ -792,7 +913,7 @@
     scratch = [
         held(TOK, D), held(TOK, D), held(TOK, D), held(D, D), held(2, TOK, D),
         held(2, 256, 256), held(2, 256, 256), held(2, 40, TOK, dtype=F32),
-        held(D, TOK, dtype=F32), held(D, TOK), held(D, TOK), held(D, TOK), held(2, D, TOK),
+        held(D, TOK, dtype=F32), held(8, 4, 48, TOK), held(D, TOK), held(D, TOK), held(2, D, TOK),
         held(16, 96, TOK), held(16, 96, TOK), held(2, 16, 2, 16, TOK),
         held(2, 4, 16, 16, TOK), held(2, 4, 16, 16, TOK), held(2, 2, 16, 2, 16, TOK),
         held(SLOTS * 32, TOK), held(ROWS, 256, dtype=F32),
@@ -803,32 +924,51 @@
         held(16, 6, 16, TOK), held(16, 6, 16, TOK),
         held(ROWS, 256, dtype=F32), held(272, 256, dtype=F32),
         held(16, 2, 2, 16, TOK), held(16, 2, 2, 16, TOK), held(16, 6, 2, 16, TOK),
-        held(8, 4, 48, TOK), held(4, 256, 768), held(4, 8, 48, 256),
+        held(TOK, D), held(TOK, D), dma((4,)), dma((6,)),
+        held(4, 8, 48, TOK), held(4, 8, 48, TOK), held(4, 256, 768), held(4, 8, 48, 256),
         held(4, 2, 48, 768), held(4, 2, 48, 768),
         held(2, 3, 16, 768), held(8, 16, 768), held(16, 768), held(3, 2, 16, 768),
-        dma((8,)), dma((8,)), dma((4, 2)), dma((4,)), dma((4, 2)), dma((4,)), dma, dma,
+        dma((8,)), dma((8,)), dma((4, 2)), dma((4,)), dma((4,)), dma((6, 4)), dma((8,)), dma((4,)),
+        dma((4,)), dma, dma,
         dma((16,)), dma((16,)), dma((16,)), dma((16,)), dma((2, 16)), dma((2, 16)),
         dma((6,)), dma((2, 4)), dma((6,)), dma((2, 4)), dma((2,)), dma((2,)), dma((2,)), dma((2,)),
         dma((8,)), dma((6,)), dma((8,)), dma((6,)), dma((16,)), dma((16,)), dma((16,)), dma((16,)),
-        dma((16,)), dma((16,)), dma((8,)), dma((6,)),
+        dma((16,)), dma((16,)), dma((10,)), dma((6,)),
         dma((4,)), dma((4,)), dma((6,)), dma((8,)), dma((8,)), dma((3, 2)),
     ]
+    anywhere = pl.BlockSpec(memory_space=pl.ANY)
+    parts = pl.pallas_call(
+        kernel,
+        out_shape=(
+            jax.ShapeDtypeStruct((TOK, D), BF16),
+            jax.ShapeDtypeStruct((TOK, D), BF16),
+            jax.ShapeDtypeStruct((16, 6, 2, 16, TOK), BF16),
+            jax.ShapeDtypeStruct((3, 2, 16, 768), BF16),
+        ),
+        in_specs=[pl.BlockSpec(memory_space=pl.ANY)] * 8,
+        out_specs=(anywhere,) * 4,
+        scratch_shapes=scratch,
+        compiler_params=pltpu.CompilerParams(
+            collective_id=0, has_side_effects=True, vmem_limit_bytes=60 * 2**20
+        ),
+    )(values[0], queries[0], out_grad[0], out_weight, filter_spec,
+      jnp.asarray(m_fwd), jnp.asarray(m_inv), jnp.asarray(twist))
     grad_query, grad_value, grad_filter, grad_weight = pl.pallas_call(
-        kernel,
+        finish,
         out_shape=(
             jax.ShapeDtypeStruct((TOK, D), BF16),
             jax.ShapeDtypeStruct((TOK, D), BF16),
             jax.ShapeDtypeStruct((2, TOK, D), F32),
             jax.ShapeDtypeStruct((24, D), F32),
         ),
-        in_specs=[pl.BlockSpec(memory_space=pl.ANY)] * 8,
-        out_specs=(vmem,) * 4,
-        scratch_shapes=scratch,
-        compiler_params=pltpu.CompilerParams(
-            collective_id=0, has_side_effects=True, vmem_limit_bytes=60 * 2**20
-        ),
-    )(values[0], queries[0], out_grad[0], out_weight, filter_spec,
-      jnp.asarray(m_fwd), jnp.asarray(m_inv), jnp.asarray(twist))
+        in_specs=[anywhere] * 4,
+        out_specs=(anywhere, anywhere, anywhere, vmem),
+        scratch_shapes=[
+            held(16, 6, 2, 16, TOK), held(3, 2, 16, 768), held(TOK, D), held(TOK, D),
+            held(2, TOK, D, dtype=F32), dma((8,)),
+        ],
+        compiler_params=pltpu.CompilerParams(vmem_limit_bytes=60 * 2**20),
+    )(*parts)
     return grad_query[None], grad_value[None], grad_filter, grad_weight
 
 

time: 104 us -> 97 us (0.933)
  local copies, waits for them, and re-layouts: 5.46 us -> 0 us
  Pallas kernels: 97.4 us -> 95.7 us
    unnamed x8 -> x0, local copies, waits for them, and re-layouts: 5.46 us -> none
    pallas_call x1, Pallas kernels: 97.4 us -> 92.2 us  [on_device(): pl.pallas_call(kernel, out_shape=(jax.ShapeDtypeStruct((TOK, D), BF16), j...]
    pallas_call x0 -> x1, Pallas kernels: none -> 3.49 us  [on_device(): pl.pallas_call(finish, out_shape=(jax.ShapeDtypeStruct((TOK, D), BF16), j...]
where the time goes in v3:
time: 97 us; the launch traced here: 96.4 us
  Pallas kernels  95.7 us (99%)
    pallas_call x1, Pallas kernels, on_device(): pl.pallas_call(kernel, out_shape=(jax.ShapeDtypeStruct((TOK, D), BF16), j...  92.2 us
    pallas_call x1, Pallas kernels, on_device(): pl.pallas_call(finish, out_shape=(jax.ShapeDtypeStruct((TOK, D), BF16), j...  3.49 us

profile of v3, /device:TPU:1, one launch (start us, length us, event | category | flops | bytes accessed | tf_op | source)
XLA Modules:
  0.0 96.4 jit_solution(13665533124736654174)
XLA Ops:
  0.6 92.2 %shard_map.111 = (bf16[128,1536]{1,0:T(8,128)(2,1)}, bf16[128,1536]{1,0:T(8,128)(2,1)}, bf16[16,6,2,16,128]{4,3,2,1,0:T(8,128)(2,1)}, bf16[3,2,16,768]{3,2,1,0:T(8,128)(2,1)}) custom-call(bf16[128,1536]{1,0:T(8,128)(2,1)} %bitcast.5, bf16[128,1536]{1,0:T(8,128)(2,1)} %bitcast.6, bf16[128,1536]{1,0:T(8,128)(2,1)} %bitcast.7, bf16[1536,1536]{1,0:T(8,128)(2,1)} %h_weight.1, ...), custom_call_target="tpu_custom_call" | custom-call | tf_op jit(solution)/shard_map/pallas_call | solution.py:940
  92.9 3.5 %shard_map.112 = (bf16[128,1536]{1,0:T(8,128)(2,1)}, bf16[128,1536]{1,0:T(8,128)(2,1)}, f32[2,128,1536]{2,1,0:T(8,128)}, f32[24,1536]{1,0:T(8,128)}) custom-call(bf16[128,1536]{1,0:T(8,128)(2,1)} %get-tuple-element.12.h_query, bf16[128,1536]{1,0:T(8,128)(2,1)} %get-tuple-element.13.h_value, bf16[16,6,2,16,128]{4,3,2,1,0:T(8,128)(2,1)} %get-tuple-element.14.h_gf, ...), custom_call_target="tpu_custom_call" | custom-call | tf_op jit(solution)/shard_map/pallas_call | solution.py:956

commit v4 on v3

--- a/solution.py
+++ b/solution.py
@@ -557,15 +557,11 @@
 
         rounds(0, 2, values_part)
 
-        def grads_part(nn):
+        def grads_spectrum(nn):
             rounds(0, 4, lambda i: landed(xg.at[nn, i], s2gr.at[nn, i]))
             transform(xg, spec_g, nn)
-            hr, hi = hs[:, :128], hs[:, 128:]
-            gr_, gi = spec_g[nn, :, :128], spec_g[nn, :, 128:]
-            untransform((gr_ * hr + gi * hi, gi * hr - gr_ * hi), ygv, nn)
-            hop_a(ygv, r2v, savs, savr, nn)
-
-        rounds(0, 2, grads_part)
+
+        rounds(0, 2, grads_spectrum)
         re, im = 0.0, 0.0
         for nn in range(2):
             vr, vi = spec_v[nn, :, :128], spec_v[nn, :, 128:]
@@ -577,61 +573,6 @@
         gp_rows = pl.ds(pl.multiple_of((1 - c) * 256, 256), 272)
         remote(gp.at[gp_rows], gpx, s_gps, s_gpr, other).start()
 
-    def mixed_share(i):
-        u = lax.rem(unit + i, 6)
-        landed(r2m.at[u], samr.at[u])
-        xx = 2 * lax.rem(x, 2) + lax.div(u, 3)
-        yh = y * 2 + lax.div(x, 2)
-        slot = mx.at[:, yh, pl.ds(pl.multiple_of(lax.rem(u, 3) * 16, 16), 16), :]
-
-        def send(j):
-            yy = lax.rem(y + j, 4)
-            src = r2m.at[u, pl.ds(yy * 4, 4)]
-            mine = jnp.logical_and(j == 0, xx == x)
-
-            @pl.when(mine)
-            def _():
-                local(src, slot, s_mxr.at[yh])
-
-            @pl.when(jnp.logical_not(mine))
-            def _():
-                remote(
-                    src, slot, s_mxs.at[u, yy], s_mxr.at[yh], at(yy * 4 + xx, z, c)
-                ).start()
-
-        rounds(0, 4, send)
-
-    def mixed_share_done(u):
-        xx = 2 * lax.rem(x, 2) + lax.div(u, 3)
-
-        def done(yy):
-            mine = jnp.logical_and(yy == y, xx == x)
-
-            @pl.when(jnp.logical_not(mine))
-            def _():
-                left(r2m.at[u, pl.ds(yy * 4, 4)], s_mxs.at[u, yy])
-
-        rounds(0, 4, done)
-
-    hop1_done(val_t, s1vs)
-    hop1_done(gm_t, s1gs)
-    over_p(lambda q: left(f_src(0, q), s1fs.at[0, q]))
-    filter_hop2_done(0)
-
-    @pl.when(two)
-    def _():
-        over_p(lambda q: left(f_src(1, q), s1fs.at[1, q]))
-        filter_hop2_done(1)
-
-    hop2_done(r1v, s2vs)
-    hop2_done(r1g, s2gs)
-    rounds(1, 8, lambda i: left(og_all.at[x, own_depth], s_ogs.at[i]))
-    rounds(1, 4, lambda i: left(qx.at[0], s_qxs.at[i]))
-
-    rounds(0, 6, mixed_share)
-
-    @pl.when(active)
-    def _():
         landed(gpx, s_gpr)
 
         def fill(i):
@@ -654,16 +595,66 @@
             lambda q: remote(gs.at[q], gr.at[p], sags.at[q], sagr.at[p], at(q, z, c)).start()
         )
 
-    rounds(0, 8, lambda i: landed(mx.at[:, i], s_mxr.at[i]))
-
-    def gate(i):
-        xx = lax.rem(x + i, 4)
-        landed(qx.at[xx], s_qxr.at[xx])
-        gat_all[xx, :, :, own_depth] = (qx[xx].astype(F32) * mx[xx].astype(F32)).astype(BF16)
-        here = gat_all.at[xx, :, :, own_depth]
-        remote(here, here, s_gxs.at[xx], s_gxr.at[xx], other).start()
-
-    rounds(0, 4, gate)
+        def grads_part(nn):
+            hr, hi = hs[:, :128], hs[:, 128:]
+            gr_, gi = spec_g[nn, :, :128], spec_g[nn, :, 128:]
+            untransform((gr_ * hr + gi * hi, gi * hr - gr_ * hi), ygv, nn)
+            hop_a(ygv, r2v, savs, savr, nn)
+
+        rounds(0, 2, grads_part)
+
+    def mixed_share(i):
+        u = lax.rem(unit + i, 6)
+        landed(r2m.at[u], samr.at[u])
+        xx = 2 * lax.rem(x, 2) + lax.div(u, 3)
+        yh = y * 2 + lax.div(x, 2)
+        slot = mx.at[:, yh, pl.ds(pl.multiple_of(lax.rem(u, 3) * 16, 16), 16), :]
+
+        def send(j):
+            yy = lax.rem(y + j, 4)
+            src = r2m.at[u, pl.ds(yy * 4, 4)]
+            mine = jnp.logical_and(j == 0, xx == x)
+
+            @pl.when(mine)
+            def _():
+                local(src, slot, s_mxr.at[yh])
+
+            @pl.when(jnp.logical_not(mine))
+            def _():
+                remote(
+                    src, slot, s_mxs.at[u, yy], s_mxr.at[yh], at(yy * 4 + xx, z, c)
+                ).start()
+
+        rounds(0, 4, send)
+
+    def mixed_share_done(u):
+        xx = 2 * lax.rem(x, 2) + lax.div(u, 3)
+
+        def done(yy):
+            mine = jnp.logical_and(yy == y, xx == x)
+
+            @pl.when(jnp.logical_not(mine))
+            def _():
+                left(r2m.at[u, pl.ds(yy * 4, 4)], s_mxs.at[u, yy])
+
+        rounds(0, 4, done)
+
+    hop1_done(val_t, s1vs)
+    hop1_done(gm_t, s1gs)
+    over_p(lambda q: left(f_src(0, q), s1fs.at[0, q]))
+    filter_hop2_done(0)
+
+    @pl.when(two)
+    def _():
+        over_p(lambda q: left(f_src(1, q), s1fs.at[1, q]))
+        filter_hop2_done(1)
+
+    hop2_done(r1v, s2vs)
+    hop2_done(r1g, s2gs)
+    rounds(1, 8, lambda i: left(og_all.at[x, own_depth], s_ogs.at[i]))
+    rounds(1, 4, lambda i: left(qx.at[0], s_qxs.at[i]))
+
+    rounds(0, 6, mixed_share)
 
     @pl.when(active)
     def _():
@@ -681,6 +672,17 @@
                 gr.at[:, half], gfi.at[:, unit], sbgs.at[k], sbgr.at[unit], at(p, zz, c)
             ).start()
 
+    rounds(0, 8, lambda i: landed(mx.at[:, i], s_mxr.at[i]))
+
+    def gate(i):
+        xx = lax.rem(x + i, 4)
+        landed(qx.at[xx], s_qxr.at[xx])
+        gat_all[xx, :, :, own_depth] = (qx[xx].astype(F32) * mx[xx].astype(F32)).astype(BF16)
+        here = gat_all.at[xx, :, :, own_depth]
+        remote(here, here, s_gxs.at[xx], s_gxr.at[xx], other).start()
+
+    rounds(0, 4, gate)
+
     mate = h * 4 + n + 1 - 2 * lax.rem(n, 2)
     passes = [
         (h * 4 + 1, n == 2), (h * 4, n == 2), (h * 4 + 3, n == 1),
@@ -741,7 +743,6 @@
 
     rounds(1, 5, weight_rows)
     hop_b(r2m, None, mix_t, sbms, sbmr)
-    hop_b(r2v, savr, gv_t, sbvs, sbvr)
     rounds(1, 4, lambda i: landed(ry.at[lax.rem(y + i, 4)], sryr.at[lax.rem(y + i, 4)]))
     total = wb[y].astype(F32)
     for i in range(1, 4):
@@ -761,6 +762,7 @@
             remote(sc.at[hh, t], rc.at[z], srcs.at[i], srcr.at[z], at(p, zz, c)).start()
 
     rounds(0, 6, rc_send)
+    hop_b(r2v, savr, gv_t, sbvs, sbvr)
     for k in range(6):
         gf_pass(k)
     rounds(0, 16, lambda q: landed(mix_t.at[q], sbmr.at[q]))

time: 97 us -> 92.1 us (0.949)
  Pallas kernels: 95.7 us -> 91.4 us
    pallas_call x1, Pallas kernels: 92.2 us -> 87.9 us  [on_device(): pl.pallas_call(kernel, out_shape=(jax.ShapeDtypeStruct((TOK, D), BF16), j...]
where the time goes in v4:
time: 92.1 us; the launch traced here: 92 us
  Pallas kernels  91.4 us (99%)
    pallas_call x1, Pallas kernels, on_device(): pl.pallas_call(kernel, out_shape=(jax.ShapeDtypeStruct((TOK, D), BF16), j...  87.9 us
    pallas_call x1, Pallas kernels, on_device(): pl.pallas_call(finish, out_shape=(jax.ShapeDtypeStruct((TOK, D), BF16), j...  3.48 us

profile of v4, /device:TPU:1, one launch (start us, length us, event | category | flops | bytes accessed | tf_op | source)
XLA Modules:
  0.0 92.0 jit_solution(10282330132945948865)
XLA Ops:
  0.6 87.9 %shard_map.111 = (bf16[128,1536]{1,0:T(8,128)(2,1)}, bf16[128,1536]{1,0:T(8,128)(2,1)}, bf16[16,6,2,16,128]{4,3,2,1,0:T(8,128)(2,1)}, bf16[3,2,16,768]{3,2,1,0:T(8,128)(2,1)}) custom-call(bf16[128,1536]{1,0:T(8,128)(2,1)} %bitcast.5, bf16[128,1536]{1,0:T(8,128)(2,1)} %bitcast.6, bf16[128,1536]{1,0:T(8,128)(2,1)} %bitcast.7, bf16[1536,1536]{1,0:T(8,128)(2,1)} %h_weight.1, ...), custom_call_target="tpu_custom_call" | custom-call | tf_op jit(solution)/shard_map/pallas_call | solution.py:942
  88.5 3.5 %shard_map.112 = (bf16[128,1536]{1,0:T(8,128)(2,1)}, bf16[128,1536]{1,0:T(8,128)(2,1)}, f32[2,128,1536]{2,1,0:T(8,128)}, f32[24,1536]{1,0:T(8,128)}) custom-call(bf16[128,1536]{1,0:T(8,128)(2,1)} %get-tuple-element.12.h_query, bf16[128,1536]{1,0:T(8,128)(2,1)} %get-tuple-element.13.h_value, bf16[16,6,2,16,128]{4,3,2,1,0:T(8,128)(2,1)} %get-tuple-element.14.h_gf, ...), custom_call_target="tpu_custom_call" | custom-call | tf_op jit(solution)/shard_map/pallas_call | solution.py:958
